TPU v7x, 32 devices: a whole 2x2x4 slice. The times are simulated.
32 devices in a mesh: acq: 4 (over y, x), strip: 8 (over z, core).
Axes of the slice: x: 2, y: 2, z: 4, core: 2. Of those that a mesh axis runs over, the one named last changes fastest.
Arguments:
- raw_echo_values: float32 [8, 8, 16, 120, 2, 512], P('strip', None, None, 'acq')
- cell_target_line: int32 [8, 8, 16], P('strip'), may hold values from -1 to 63, as said below
- cell_track_displacement: int32 [8, 8, 16], P('strip'), may hold values from -48 to 48
- along_track_chirp_slope: float32 [120], P('acq'), may hold values from 0.001 to 0.01
- along_track_look_radius: int32 [64], P('strip'), may hold values from 5 to 7
- range_look_radius: int32 [64], replicated, may hold values from 3 to 7
Outputs:
- coherence: float32 [120, 120, 2, 4096], P('acq', None, None, 'strip')
Inputs may be any that keep to these rules, and one draw needn't show every extreme that they name: `cell_target_line`: in each reader's group of 16 slots for one strip the live slots come first; every row of every strip is named by at least one slot; some groups are full.
All inputs are finite; a program needn't handle non-finite values.
Results may differ from a plain program's by a relative error of at most 0.00065.
Values may be sent and summed in bfloat16 or wider, within the bound.
No kernel may reach another device: no remote copies, remote signals or barrier semaphores. Data moves between devices by JAX's collectives and lax.ppermute only.
A program may use at most 320 MiB of HBM per device.

v0:
```python
import jax
import jax.numpy as jnp
from jax import lax
from jax.sharding import PartitionSpec as P

epsilon = 1e-06


def extended(value, sides, width):
    for axis, dim in sides:
        devices, length = (lax.axis_size(axis), value.shape[dim])
        up = [(i, (i + 1) % devices) for i in range(devices - 1)]
        down = [(j, i) for i, j in up]
        last = lax.slice_in_dim(value, length - width, length, axis=dim)
        initial = lax.slice_in_dim(value, 0, width, axis=dim)
        before = lax.ppermute(last, axis, up)
        after = lax.ppermute(initial, axis, down)
        value = jnp.concatenate([before, value, after], axis=dim)
    return value


def subtract_linear_chirp(raw_echo_values, cell_track_displacement, along_track_chirp_slope):
    squared = cell_track_displacement.astype(jnp.float32) ** 2
    phase = squared[..., None] * along_track_chirp_slope
    cosine = jnp.cos(phase)[..., None]
    sine_part = jnp.sin(phase)[..., None]
    inphase_source = raw_echo_values[..., 0, :]
    quadrature_source = raw_echo_values[..., 1, :]
    real_out = inphase_source * cosine + quadrature_source * sine_part
    imag_out = quadrature_source * cosine - inphase_source * sine_part
    return jnp.stack([real_out, imag_out], axis=-2)


def windows_of(padded):
    inner = padded.shape[2] - 8
    acq_count = padded.shape[0]
    columns = padded.shape[3]
    upper = padded[:, :, :inner].reshape(acq_count, 2, inner // 8, 8, columns)
    lower = padded[:, :, 8:].reshape(acq_count, 2, inner // 8, 8, columns)
    return jnp.concatenate([upper, lower], axis=3)


def look(values, colmask):
    return jnp.einsum("...c,cq->...q", values, colmask, precision=lax.Precision.HIGHEST)


def power_of(win, weight):
    weighted = win * weight[None, None, :, :, None]
    total = None
    for part_index in range(2):
        for offset_index in range(16):
            left_rows = weighted[:, part_index, :, offset_index, :].astype(jnp.float32)
            right_rows = win[:, part_index, :, offset_index, :].astype(jnp.float32)
            term = left_rows * right_rows
            total = term if total is None else total + term
    return total


def pair_sums(weighted, right_win):
    real_sum = None
    imag_sum = None
    for offset_index in range(16):
        left_real = weighted[:, 0, :, offset_index, :].astype(jnp.float32)[:, None]
        left_imag = weighted[:, 1, :, offset_index, :].astype(jnp.float32)[:, None]
        right_real = right_win[:, 0, :, offset_index, :].astype(jnp.float32)[None]
        right_imag = right_win[:, 1, :, offset_index, :].astype(jnp.float32)[None]
        real_term = left_real * right_real + left_imag * right_imag
        imag_term = left_imag * right_real - left_real * right_imag
        real_sum = real_term if real_sum is None else real_sum + real_term
        imag_sum = imag_term if imag_sum is None else imag_sum + imag_term
    return (real_sum, imag_sum)


def coherence_block(left_win, left_power, right_win, weight, colmask):
    weighted = left_win * weight[None, None, :, :, None]
    real_sum, imag_sum = pair_sums(weighted, right_win)
    right_power = look(power_of(right_win, weight), colmask)
    scale = 1.0 / jnp.sqrt(left_power[:, None] * right_power[None] + epsilon)
    real_look = look(real_sum, colmask) * scale
    imag_look = look(imag_sum, colmask) * scale
    stacked = jnp.stack([real_look, imag_look], axis=2)
    return stacked.reshape(stacked.shape[0], stacked.shape[1], 2, -1)


def per_device(
    raw_echo_values,
    cell_target_line,
    cell_track_displacement,
    along_track_chirp_slope,
    along_track_look_radius,
    range_look_radius,
):
    received, rows_in, offsets_in = (
        lax.all_to_all(raw_echo_values, "strip", split_axis=1, concat_axis=0, tiled=True),
        lax.all_to_all(cell_target_line, "strip", split_axis=1, concat_axis=0, tiled=True),
        lax.all_to_all(cell_track_displacement, "strip", split_axis=1, concat_axis=0, tiled=True),
    )
    levelled_echoes = subtract_linear_chirp(received, offsets_in, along_track_chirp_slope).astype(
        jnp.bfloat16
    )
    columns = levelled_echoes.shape[5]
    strip_rows = along_track_look_radius.shape[0] * 8
    out_cols = range_look_radius.shape[0]
    selector = rows_in[None] == jnp.arange(strip_rows, dtype=jnp.int32)[:, None, None, None]
    counts = jnp.sum(selector.astype(jnp.float32), axis=(1, 2, 3))
    onehot = selector.astype(jnp.bfloat16)
    summed = jnp.einsum(
        "xrdk,rdkapc->apxc", onehot, levelled_echoes, preferred_element_type=jnp.float32
    )
    tile = (summed / counts[None, None, :, None]).astype(jnp.bfloat16)
    padded = extended(tile, (("strip", 2),), 4)
    offsets_row = jnp.abs(jnp.arange(16, dtype=jnp.int32) - 8)
    weight = (offsets_row[None, :] <= along_track_look_radius[:, None]).astype(jnp.bfloat16)
    centres = 8 * jnp.arange(out_cols, dtype=jnp.int32) + 4
    distance = jnp.abs(jnp.arange(columns, dtype=jnp.int32)[:, None] - centres[None, :])
    colmask = (distance <= range_look_radius[None, :]).astype(jnp.float32)
    local_win = windows_of(padded)
    local_power = look(power_of(local_win, weight), colmask)
    return coherence_block(
        local_win,
        local_power,
        windows_of(lax.all_gather(padded, "acq", axis=0, tiled=True)),
        weight,
        colmask,
    )


def solution(mesh):
    placed = (
        P("strip", None, None, "acq", None, None),
        P("strip", None, None),
        P("strip", None, None),
        P("acq"),
        P("strip"),
        P(),
    )
    return jax.shard_map(
        per_device,
        mesh=mesh,
        in_specs=placed,
        out_specs=P("acq", None, None, "strip"),
        check_vma=False,
    )
```

profile of v0, /device:TPU:0, one launch (start us, length us, event | category | flops | bytes accessed | tf_op | source)
XLA Modules:
  0.0 1439.4 jit_solution(14875836102643587524)
XLA Ops:
  6.5 11.8 all_to_all.30
  18.3 3.3 all-to-all-start.2
  21.7 15.7 %copy.229 = f32[1,8,16,30,2,512]{5,2,3,4,0,1:T(8,128)} copy(f32[1,8,16,30,2,512]{5,4,3,2,1,0:T(2,128)} %param.6) | data formatting | bytes 31457280 | tf_op args[0]
  37.3 5.8 all-to-all-start
  43.8 340.5 %all-to-all-done = f32[1,8,16,30,2,512]{5,2,3,4,0,1:T(8,128)} async-done(((f32[1,8,16,30,2,512]{5,2,3,4,0,1:T(8,128)}), f32[1,8,16,30,2,512]{5,2,3,4,0,1:T(8,128)}, u32[]{:S(2)}, u32[]{:S(2)}) %all-to-all-start) | async-done | bytes 15728672 | tf_op jit(solution)/shard_map/all_to_all | solution.py:94
  384.3 14.8 %copy.310 = f32[1,8,16,30,2,512]{5,2,1,3,4,0:T(8,128)} copy(f32[1,8,16,30,2,512]{5,2,3,4,0,1:T(8,128)} %all-to-all-done) | data formatting | bytes 31457280 | tf_op jit(solution)/shard_map/all_to_all | solution.py:94
  399.1 6.7 fusion.267
  405.8 2.5 fusion.271
  408.5 1.6 collective-permute-start
  411.6 1.9 collective-permute-done.1
  413.4 3.9 pad_maximum_fusion.1
  418.9 7.8 fusion.270
  426.7 3.9 copy.235
  430.6 3.4 copy.236
  434.0 8.7 maximum_multiply_fusion.1
  442.8 4.9 fusion.494
  449.0 3.6 fusion.495
  452.6 5.7 fusion.370
  458.3 129.2 %all-gather.2.cloned.1.call-done = bf16[120,2,72,512]{3,2,1,0:T(8,128)(2,1)} async-done(((bf16[30,2,72,512]{3,2,1,0:T(8,128)(2,1)}), bf16[120,2,72,512]{3,2,1,0:T(8,128)(2,1)}) %all-gather.2.cloned.1.call-update) | async-done | bytes 17694736 | tf_op jit(solution)/shard_map/all_gather | solution.py:122
  587.5 11.7 slice_bitcast_fusion.1
  599.2 11.3 copy.237
  610.5 11.7 copy.253
  622.2 14.0 fusion.368
  636.2 21.4 %maximum_multiply_fusion = bf16[120,2,8,16,512]{4,2,0,3,1:T(8,128)(2,1)} fusion(bf16[120,2,8,8,512]{4,2,0,3,1:T(8,128)(2,1)} %copy.253, bf16[120,2,8,8,512]{4,2,0,3,1:T(8,128)(2,1)} %copy.237, bf16[8,16]{0,1:T(8,128)(2,1)S(1)} %compare_convert_fusion), kind=kLoop, calls=%fused_computation.128 | loop fusion | flops 31457280 | bytes 62914816 | tf_op jit(solution)/shard_map/mul | solution.py:48
  657.6 14.5 %fusion.352 = (f32[120,8,512]{2,1,0:T(8,128)}, f32[120,8,512]{2,1,0:T(8,128)}, f32[120,8,512]{2,1,0:T(8,128)}, f32[120,8,512]{2,1,0:T(8,128)}, f32[120,8,512]{2,...) fusion(bf16[120,2,8,8,512]{4,2,0,3,1:T(8,128)(2,1)} %copy.253), kind=kLoop, calls=%fused_computation.408 | loop fusion | flops 7864320 | bytes 47185920 | tf_op jit(solution)/shard_map/convert_element_type | solution.py:65
  672.1 21.9 %fusion.275 = f32[120,8,64]{2,1,0:T(8,128)S(1)} fusion(bf16[120,2,8,16,512]{4,2,0,3,1:T(8,128)(2,1)} %maximum_multiply_fusion, bf16[120,2,8,8,512]{4,2,0,3,1:T(8,128)(2,1)} %copy.237, bf16[120,2,8,8,512]{4,2,0,3,1:T(8,128)(2,1)} %copy.253, s32[64]{0:T(128)S(1)} %copy-done.3, s32[64]{0:T(128)S(1)} %multiply_add_fusion), kind=kOutput, calls=%fused_computation.283 | convolution fusion | flops 440008704 | bytes 63160832 | tf_op jit(solution)/shard_map/...c,cq->...q/dot_general | solution.py:44
  694.0 328.4 %fusion.257 = f32[30,120,8,64]{3,2,1,0:T(8,128)} fusion(f32[120,8,512]{2,1,0:T(8,128)} %get-tuple-element.26, f32[30,8,512]{2,1,0:T(8,128)} %get-tuple-element.42, f32[120,8,512]{2,1,0:T(8,128)} %get-tuple-element.27, f32[30,8,512]{2,1,0:T(8,128)} %get-tuple-element.43, f32[120,8,512]{2,1,0:T(8,128)} %get-tuple-element.28, ...), kind=kOutput, calls=%fused_computation.263 | convolution fusion | flops 12259123200 | bytes 86355968 | tf_op jit(solution)/shard_map/...c,cq->...q/dot_general | solution.py:44
  1022.4 12.1 copy.303
  1034.5 352.0 %fusion.256 = f32[30,120,8,64]{3,2,1,0:T(8,128)} fusion(f32[120,8,512]{2,1,0:T(8,128)} %get-tuple-element.26, f32[30,8,512]{2,1,0:T(8,128)} %get-tuple-element.42, f32[120,8,512]{2,1,0:T(8,128)} %get-tuple-element.27, f32[30,8,512]{2,1,0:T(8,128)} %get-tuple-element.43, f32[120,8,512]{2,1,0:T(8,128)} %get-tuple-element.28, ...), kind=kOutput, calls=%fused_computation.262 | convolution fusion | flops 12259123200 | bytes 86355968 | tf_op jit(solution)/shard_map/...c,cq->...q/dot_general | solution.py:44
  1386.5 12.1 copy.304
  1398.7 12.9 pad_maximum_fusion
  1411.5 20.6 %copy.305 = f32[30,120,2,512]{3,2,1,0:T(2,128)} copy(f32[30,120,2,512]{1,3,0,2:T(8,128)} %pad_maximum_fusion) | data formatting | bytes 29491200 | tf_op jit(solution)/shard_map/stack | solution.py:81
  (26 shorter events, 5.2 us)
Async XLA Ops:
  18.3 19.0 %all-to-all-start.2 = ((s32[1,8,16]{2,0,1:T(1,128)}), s32[1,8,16]{2,0,1:T(1,128)S(1)}, u32[]{:S(2)}, u32[]{:S(2)}) async-start(s32[1,8,16]{2,0,1:T(1,128)} %bitcast.964), calls=%async_computation.2 | async-start | bytes 8192 | tf_op jit(solution)/shard_map/all_to_all | solution.py:95
  37.3 5.9 copy-start.4
  37.3 347.0 %all-to-all-start = ((f32[1,8,16,30,2,512]{5,2,3,4,0,1:T(8,128)}), f32[1,8,16,30,2,512]{5,2,3,4,0,1:T(8,128)}, u32[]{:S(2)}, u32[]{:S(2)}) async-start(f32[1,8,16,30,2,512]{5,2,3,4,0,1:T(8,128)} %copy.229), calls=%async_computation | async-start | bytes 31457280 | tf_op jit(solution)/shard_map/all_to_all | solution.py:94
  43.1 544.3 %all-gather.2.cloned.1.call-start = ((), (), s32[]{:S(2)}) async-start(), calls=%async_computation.3 | async-start | bytes 22118400 | tf_op jit(solution)/shard_map/all_gather | solution.py:122
  408.3 5.2 copy-start.1
  408.5 3.1 collective-permute-start
  410.0 3.4 collective-permute-start.1
  417.4 0.7 copy-start.5
  417.4 0.7 copy-start.3
  442.8 6.2 copy-start
  1022.4 12.1 copy-start.2
Sparse Core Ops, SparseCore 0:
  417.5 169.8 all-gather.1
where the time goes:
time: 1450 us; the launch traced here: 1440 us
  matrix products  710 us (49%)
  waiting for transfers between devices  472 us (33%)
  local copies, waits for them, and re-layouts  119 us (8%)
  other arithmetic  99.9 us (7%)
    dot_general x4, matrix products, look(): jnp.einsum('...c,cq->...q', values, colmask, precision=lax.Precision.HIGH...  708 us
    all_to_all x1, waiting for transfers between devices, per_device(): lax.all_to_all(raw_echo_values, 'strip', split_axis=1, concat_axis=0, til...  341 us
    all_gather x1, waiting for transfers between devices, per_device(): lax.all_gather(padded, 'acq', axis=0, tiled=True)  129 us
  transfers between devices with their start and end apart: 5, of which 3 were waited for; matrix products, arithmetic and copies ran while one was open for 4% of the time, Pallas kernels for 0%

commit v1 on v0

v1 whole, which is shorter than its diff:
```python
import functools

import jax
import jax.numpy as jnp
from jax import lax
from jax.experimental import pallas as pl
from jax.experimental.pallas import tpu as pltpu
from jax.sharding import PartitionSpec as P

epsilon = 1e-06
LANES = 128
F32 = jnp.float32
BF16 = jnp.bfloat16


def work(microseconds):
    return pl.CostEstimate(
        flops=int(microseconds * 1e9), bytes_accessed=int(microseconds * 1e6), transcendentals=0
    )


def params(**more):
    return pltpu.CompilerParams(vmem_limit_bytes=56 * 1024 * 1024, **more)


def sublane_exchange(arrays, row, wanted):
    known = {}

    def value(level, i):
        if level == 0:
            return arrays[i]
        if (level, i) not in known:
            step = 8 >> level
            keep = (row // step) % 2 == (1 if i & step else 0)
            shift = 8 - step if i & step else step
            other = pltpu.roll(value(level - 1, i ^ step), shift, 0)
            known[level, i] = jnp.where(keep, value(level - 1, i), other)
        return known[level, i]

    return [value(3, i) for i in wanted]


def deramp_kernel(acqs, chosen, with_lines, *refs):
    raw_ref, cos_ref, sin_ref = refs[:3]
    lines_ref = refs[3] if with_lines else None
    outs = refs[4:] if with_lines else refs[3:]
    cap = cos_ref.shape[1]
    row = lax.broadcasted_iota(jnp.int32, (8, LANES), 0)
    wanted = [2 * g + part for g in chosen for part in range(2)]
    cosines = cos_ref[0]
    sines = sin_ref[0]
    for a in range(acqs):
        halves = []
        for first in range(0, cap, 8):
            cosine = jnp.broadcast_to(cosines[first : first + 8, a : a + 1], (8, LANES))
            sine = jnp.broadcast_to(sines[first : first + 8, a : a + 1], (8, LANES))
            if len(wanted) == 2:
                values = [
                    raw_ref[pl.ds((first * acqs + a) * 8 + w, 8, stride=acqs * 8), :]
                    for w in wanted
                ]
            else:
                starts = [((first + i) * acqs + a) * 8 for i in range(8)]
                loaded = [raw_ref[start : start + 8, :] for start in starts]
                values = sublane_exchange(loaded, row, wanted)
            done = []
            for real, imag in zip(values[::2], values[1::2]):
                done += [real * cosine + imag * sine, imag * cosine - real * sine]
            halves.append(done)
        for index, out in enumerate(outs):
            for part in range(2):
                pieces = [half[2 * index + part] for half in halves]
                out[0, part * acqs + a] = jnp.concatenate(pieces, axis=0).astype(BF16)
    if with_lines:
        lines = lines_ref[pl.ds(pl.program_id(0), 1), :].astype(F32)
        slot = lax.broadcasted_iota(jnp.int32, (cap, cap), 0)
        same = slot == lax.broadcasted_iota(jnp.int32, (cap, cap), 1)
        lines = jnp.sum(jnp.where(same, lines, 0.0), axis=1, keepdims=True)
        lines = jnp.broadcast_to(lines, (cap, LANES))
        outs[0][0, 2 * acqs] = lines.astype(BF16)


def deramp(raw, cosine, sine, chosen, lines=None):
    _, strips, cap, acqs, _, columns = raw.shape
    groups = columns // LANES
    view = raw.reshape(strips * cap, acqs, 2, groups, LANES)
    view = view.transpose(0, 1, 3, 2, 4).reshape(strips * cap * acqs * groups * 2, LANES)
    block = cap * acqs * groups * 2
    pieces = 2 * acqs + (lines is not None)
    out = jax.ShapeDtypeStruct((strips, pieces, cap, LANES), BF16)
    args = [view, cosine, sine]
    in_specs = [
        pl.BlockSpec((block, LANES), lambda i: (i, 0)),
        pl.BlockSpec((1, cap, acqs), lambda i: (i, 0, 0)),
        pl.BlockSpec((1, cap, acqs), lambda i: (i, 0, 0)),
    ]
    if lines is not None:
        args.append(lines)
        in_specs.append(pl.BlockSpec((strips, cap), lambda i: (0, 0)))
    return pl.pallas_call(
        functools.partial(deramp_kernel, acqs, chosen, lines is not None),
        grid=(strips,),
        in_specs=in_specs,
        out_specs=[pl.BlockSpec((1, pieces, cap, LANES), lambda i: (i, 0, 0, 0))] * len(chosen),
        out_shape=[out] * len(chosen),
        compiler_params=params(),
        name=f"deramp{chosen[0]}",
        cost_estimate=work(6 if lines is not None else 9),
    )(*args)


def tile_kernel(acqs, padded, lines_ref, data_ref, out_ref, top_ref, bottom_ref, scratch):
    readers, _, cap, _ = data_ref.shape
    slots = readers * cap
    strip_rows = out_ref.shape[0]

    def piece(ref, index):
        value = ref[:, index]
        if cap % 16:
            return value.astype(F32).reshape(slots, LANES).astype(BF16)
        return value.reshape(slots, LANES)

    target = lax.broadcasted_iota(jnp.int32, (slots, LANES), 1).astype(F32)
    selector = jnp.where(piece(lines_ref, 0).astype(F32) == target, 1.0, 0.0)
    selector = selector.astype(F32).T[:strip_rows]
    counts = jnp.broadcast_to(
        jnp.sum(selector, axis=1, keepdims=True), (strip_rows, LANES)
    )
    onehot = selector.astype(BF16)
    zeros = jnp.zeros((strip_rows, LANES), F32)
    for part in range(2):
        for a in range(acqs):
            summed = jnp.dot(
                onehot, piece(data_ref, part * acqs + a), preferred_element_type=F32
            )
            scratch[pl.ds(part * padded + a, strip_rows, stride=2 * padded), :] = pltpu.roll(
                summed / counts, 4, 1
            )
        for a in range(acqs, padded):
            scratch[pl.ds(part * padded + a, strip_rows, stride=2 * padded), :] = zeros
    for x in range(strip_rows):
        value = scratch[pl.ds(x * 2 * padded, 2 * padded), :].astype(BF16)
        out_ref[x] = value
        if x < 4:
            top_ref[x] = value
        if x >= strip_rows - 4:
            bottom_ref[x - strip_rows + 4] = value


def make_tile(lines, data, acqs, padded, strip_rows):
    readers, pieces, cap, _ = data.shape
    whole = (readers, pieces, cap, LANES)
    return pl.pallas_call(
        functools.partial(tile_kernel, acqs, padded),
        grid=(1,),
        in_specs=[
            pl.BlockSpec((readers, 1, cap, LANES), lambda i: (0, 2 * acqs, 0, 0)),
            pl.BlockSpec(whole, lambda i: (0, 0, 0, 0)),
        ],
        out_specs=[
            pl.BlockSpec((n, 2 * padded, LANES), lambda i: (0, 0, 0)) for n in (strip_rows, 4, 4)
        ],
        out_shape=[
            jax.ShapeDtypeStruct((n, 2 * padded, LANES), BF16) for n in (strip_rows, 4, 4)
        ],
        scratch_shapes=[pltpu.VMEM((strip_rows * 2 * padded, LANES), F32)],
        compiler_params=params(),
        name="tile",
        cost_estimate=work(4),
    )(lines, data)


def block_exchange(arrays, lane):
    arrays = list(arrays)
    for step in (4, 2, 1):
        mask = (lane // (16 * step)) % 2 == 0
        new = list(arrays)
        for i in range(8):
            if i & step:
                continue
            low, high = arrays[i], arrays[i + step]
            new[i] = jnp.where(mask, low, pltpu.roll(high, 16 * step, 1))
            new[i + step] = jnp.where(
                mask, pltpu.roll(low, LANES - 16 * step, 1), high
            )
        arrays = new
    return arrays


def pairs_kernel(k, last, sources, padded, *refs):
    refs = list(refs)
    radius_ref, mask_ref, cmask_ref = refs[:3]
    del refs[:3]
    halos = refs[: len(sources[0])]
    del refs[: len(sources[0])]
    count = 1 + max(index for part in sources for index, _ in part)
    blocks = refs[: 2 * count]
    del refs[: 2 * count]
    first = k == 0
    edge_ref = None
    if not first:
        before = refs[:2]
        before_halo_ref, edge_ref = refs[2:4]
        del refs[:5]
    sums_ref = refs.pop(0)
    edge_out = None if last else refs.pop(0)
    even, odd, over, left, left_over, power, staged, sems = refs

    y = pl.program_id(0)
    out_rows = radius_ref.shape[0]
    rows2 = 2 * padded
    width = 2 * LANES
    slots = 17 if last else 16
    low = 1 if first else 0
    q0 = 16 * k - 1 + low
    lane = lax.broadcasted_iota(jnp.int32, (rows2, LANES), 1)
    early = lax.broadcasted_iota(jnp.int32, (8, width), 0) < 4

    def weight(o, j):
        o = jnp.clip(o, 0, out_rows - 1)
        return jnp.where(radius_ref[o] >= abs(j - 8), 1.0, 0.0).astype(F32)

    def squares(value):
        return value[:, :LANES] * value[:, :LANES] + value[:, LANES:] * value[:, LANES:]

    at_top = y == 0
    at_bottom = y == out_rows

    def rows_of(low_ref, high_ref, halo, xx, size):
        main = low_ref[xx, size, :] if xx < 4 else high_ref[xx - 4, size, :]
        edge = at_top if xx < 4 else at_bottom
        return jnp.where(edge, halo.astype(F32), main.astype(F32))

    slot_now = lax.rem(y, 2)
    slot_old = 1 - slot_now
    for xx in range(8):
        x = y * 8 + xx
        parts = []
        for number, part in enumerate(sources):
            pieces = [
                rows_of(
                    blocks[2 * index],
                    blocks[2 * index + 1],
                    halos[i][xx, number * padded : (number + 1) * padded, :],
                    xx,
                    slice(offset, offset + padded),
                )
                for i, (index, offset) in enumerate(part)
            ]
            parts.append(jnp.concatenate(pieces, axis=0).T)
        value = jnp.concatenate(parts, axis=1)
        top = value[:8]
        bottom = value[LANES - 8 :]
        if first:
            tail = jnp.zeros((8, width), F32)
            proper = value
        else:
            tail = edge_ref[xx, :8]
            start = jnp.where(early, edge_ref[xx, 8:], top)
            proper = jnp.concatenate([start, value[8:]], axis=0)
        even[x] = proper.reshape(8, 16, width).astype(BF16)
        shifted = jnp.concatenate([tail, proper[: LANES - 8]], axis=0)
        odd[x] = shifted.reshape(8, 16, width).astype(BF16)
        levels = [squares(tail), squares(proper)]
        if last:
            over[x] = jnp.concatenate([bottom, top], axis=0).astype(BF16)
            levels.append(squares(top))
        else:
            edge_out[xx, :8] = bottom
            edge_out[xx, 8:] = top
        level = jnp.concatenate(levels, axis=0)
        new = weight(y, xx) * level
        old = weight(y - 1, xx + 8) * level
        if xx == 0:
            power[slot_now] = new
        else:
            power[slot_now] = power[slot_now] + new
        power[slot_old] = power[slot_old] + old

    raw = [
        rows_of(blocks[0], blocks[1], halos[0][xx], xx, slice(None)) for xx in range(8)
    ]
    owned = raw
    rolled = [pltpu.roll(value, 8, 1) for value in owned]
    if not first:
        before = [
            rows_of(before[0], before[1], before_halo_ref[xx], xx, slice(None))
            for xx in range(8)
        ]
        owned = [jnp.where(lane < 4, before[xx], raw[xx]) for xx in range(8)]
        rolled = [pltpu.roll(value, 8, 1) for value in owned]
        rolled = [
            jnp.where(lane < 8, pltpu.roll(before[xx], 8, 1), rolled[xx]) for xx in range(8)
        ]
    for tile, value in enumerate(block_exchange(owned, lane)):
        left[slot_now, 0, tile] = value
    for tile, value in enumerate(block_exchange(rolled, lane)):
        left[slot_now, 1, tile] = value
    if last:
        total = None
        for xx in range(8):
            value = pltpu.roll(raw[xx], 8 + 16 * xx, 1)
            total = value if total is None else jnp.where(lane // 16 == xx, value, total)
        left_over[slot_now] = total

    @pl.when(y > 0)
    def _():
        o = y - 1
        buffer = lax.rem(o, 2)

        def send(row, which):
            return pltpu.make_async_copy(
                staged.at[which, pl.ds(low, slots - low)],
                sums_ref.at[row, pl.ds(q0, slots - low)],
                sems.at[which],
            )

        @pl.when(o >= 2)
        def _():
            send(o - 2, buffer).wait()

        for i in range(low, slots):
            if i == 16:
                right = over[pl.ds(o * 8, 16)].reshape(256, width)
                sides = [left_over[slot_old], left_over[slot_now]]
            else:
                tile, shift = (i // 2, 1) if i % 2 == 0 else ((i - 1) // 2, 0)
                source = odd if shift else even
                right = source[pl.ds(o * 8, 16), tile].reshape(256, width)
                sides = [left[slot_old, shift, tile], left[slot_now, shift, tile]]
            row = 16 * k + i
            mask = mask_ref[0, row : row + 1, :]
            weighted = (jnp.concatenate(sides, axis=1) * mask).astype(BF16)
            product = jnp.dot(weighted, right, preferred_element_type=F32)
            real = product[:padded, :LANES] + product[padded:, LANES:]
            imag = product[padded:, :LANES] - product[:padded, LANES:]
            energy = jnp.sum(
                cmask_ref[row] * power[slot_old, pl.ds(8 * i, 16), :], axis=0, keepdims=True
            )
            staged[buffer, i, :padded] = real
            staged[buffer, i, padded:] = imag
            staged[buffer, i, padded - 1 : padded] = energy
        send(o, buffer).start()

        @pl.when(o == out_rows - 1)
        def _():
            if out_rows > 1:
                send(o - 1, 1 - buffer).wait()
            send(o, buffer).wait()


def pair_sums(
    k, last, radius, mask, cmask, halos, blocks, sources, before, before_halo, edge, sums
):
    strip_rows, rows2, _ = blocks[0].shape
    rows = strip_rows + 8
    padded = rows2 // 2
    width = 2 * LANES
    out_rows = radius.shape[0]
    first = k == 0
    top = strip_rows // 4 - 1

    def by_rows(array):
        return pl.BlockSpec((8, *array.shape[1:]), lambda y: (y, 0, 0))

    def by_halves(array):
        block = (4, *array.shape[1:])
        return [
            pl.BlockSpec(block, lambda y: (jnp.maximum(2 * y - 1, 0), 0, 0)),
            pl.BlockSpec(block, lambda y: (jnp.minimum(2 * y, top), 0, 0)),
        ]

    def whole(array):
        return pl.BlockSpec(array.shape, lambda y: (0,) * array.ndim)

    edge_shape = jax.ShapeDtypeStruct((rows, 16, width), F32)
    args = [radius, mask, cmask, *halos]
    in_specs = [
        pl.BlockSpec(memory_space=pltpu.SMEM),
        pl.BlockSpec((1, *mask.shape[1:]), lambda y: (jnp.maximum(y - 1, 0), 0, 0)),
        whole(cmask),
        *[whole(halo) for halo in halos],
    ]
    for block in blocks:
        args += [block, block]
        in_specs += by_halves(block)
    if not first:
        args += [before, before, before_halo, edge]
        in_specs += [*by_halves(before), whole(before_halo), by_rows(edge)]
    aliases = {}
    if not first:
        args.append(sums)
        in_specs.append(pl.BlockSpec(memory_space=pl.ANY))
        aliases[len(args) - 1] = 0
    out_cols = cmask.shape[0] - 1
    out_shape = [jax.ShapeDtypeStruct((out_rows, out_cols, rows2, LANES), F32)]
    out_specs = [pl.BlockSpec(memory_space=pl.ANY)]
    if not last:
        out_shape.append(edge_shape)
        out_specs.append(by_rows(edge_shape))
    outs = pl.pallas_call(
        functools.partial(pairs_kernel, k, last, sources, padded),
        grid=(rows // 8,),
        in_specs=in_specs,
        out_specs=out_specs,
        out_shape=out_shape,
        input_output_aliases=aliases,
        scratch_shapes=[
            pltpu.VMEM((rows, 8, 16, width), BF16),
            pltpu.VMEM((rows, 8, 16, width), BF16),
            pltpu.VMEM((rows if last else 8, 16, width), BF16),
            pltpu.VMEM((2, 2, 8, rows2, LANES), F32),
            pltpu.VMEM((2, rows2, LANES), F32),
            pltpu.VMEM((2, 144 if last else 136, LANES), F32),
            pltpu.VMEM((2, 17, rows2, LANES), F32),
            pltpu.SemaphoreType.DMA((2,)),
        ],
        compiler_params=params(),
        name=f"pairs{k}",
        cost_estimate=work(16),
    )(*args)
    return (outs[0], None) if last else (outs[0], outs[1])


def finish_kernel(acqs, padded, groups, me_ref, real_ref, imag_ref, energy_ref, out_ref, power):
    step = pl.program_id(0)
    me = me_ref[0]
    out_rows, out_cols, _, _ = real_ref.shape
    pixels = out_rows * out_cols
    lane_groups = pixels // LANES

    def strided(ref, g, row):
        return ref.reshape(pixels * 8, LANES)[pl.ds(g * LANES * 8 + row, LANES, stride=8), :]

    @pl.when(step == 0)
    def _():
        for g in range(lane_groups):
            power[g] = strided(energy_ref, g, 7).T

    for m in range(8):
        for g in range(lane_groups):
            mine = power[g, pl.ds(step * 8 + m, 1), :]
            scale = lax.rsqrt(power[g] * mine + epsilon)
            for part, ref in enumerate((real_ref, imag_ref)):
                value = strided(ref, g, m).T * scale
                for i in range(groups):
                    start = lax.bitwise_xor(me, i) * (acqs * 2 * lane_groups)
                    out_ref[
                        m, pl.ds(start + 2 * g + part, acqs, stride=2 * lane_groups), :
                    ] = value[i * padded : i * padded + acqs]


def finish(me, sums, acqs, groups):
    out_rows, out_cols, rows2, _ = sums.shape
    padded = rows2 // 2
    lane_groups = out_rows * out_cols // LANES
    total = acqs * groups
    blocks = padded // 8

    def spec(index):
        return pl.BlockSpec((out_rows, out_cols, 8, LANES), index)

    out = pl.pallas_call(
        functools.partial(finish_kernel, acqs, padded, groups),
        grid=(pl.cdiv(acqs, 8),),
        in_specs=[
            pl.BlockSpec(memory_space=pltpu.SMEM),
            spec(lambda i: (0, 0, i, 0)),
            spec(lambda i: (0, 0, i + blocks, 0)),
            spec(lambda i: (0, 0, blocks - 1, 0)),
        ],
        out_specs=pl.BlockSpec((8, total * 2 * lane_groups, LANES), lambda i: (i, 0, 0)),
        out_shape=jax.ShapeDtypeStruct((acqs, total * 2 * lane_groups, LANES), F32),
        scratch_shapes=[pltpu.VMEM((lane_groups, LANES, LANES), F32)],
        compiler_params=params(),
        name="finish",
        cost_estimate=pl.CostEstimate(
            flops=6 * sums.size, bytes_accessed=8 * sums.size, transcendentals=sums.size // 2
        ),
    )(me, sums, sums, sums)
    out = out.reshape(acqs, total, lane_groups, 2, LANES).transpose(0, 1, 3, 2, 4)
    return out.reshape(acqs, total, 2, lane_groups * LANES)


def exchange(value, axis, bit):
    size = lax.axis_size(axis)
    return lax.ppermute(value, axis, [(i, i ^ bit) for i in range(size)])


def neighbours(top, bottom):
    devices = lax.axis_size("strip")
    up = [(i, i + 1) for i in range(devices - 1)]
    down = [(j, i) for i, j in up]
    before = lax.ppermute(bottom, "strip", up)
    after = lax.ppermute(top, "strip", down)
    return jnp.concatenate([before, after], axis=0)


def after(value, *others):
    return lax.optimization_barrier((value, *others))[0]


def gathered(own, padded, filler=()):
    groups = lax.axis_size("acq")
    if groups != 4:
        blocks = [own] + [exchange(own, "acq", bit) for bit in range(1, groups)]
        return blocks, [[(i, part * padded) for i in range(groups)] for part in range(2)]
    one = exchange(own, "acq", 1)
    two = exchange(own, "acq", 2)
    real = exchange(after(two[:, :padded], *filler), "acq", 1)
    imag = exchange(after(one[:, padded:], *filler), "acq", 2)
    blocks = [own, one, two, real, imag]
    shared = [[(i, part * padded) for i in range(3)] for part in range(2)]
    return blocks, [shared[0] + [(3, 0)], shared[1] + [(4, 0)]]


def per_device(
    raw_echo_values,
    cell_target_line,
    cell_track_displacement,
    along_track_chirp_slope,
    along_track_look_radius,
    range_look_radius,
):
    _, strips, cap, acqs, _, columns = raw_echo_values.shape
    groups = lax.axis_size("acq")
    padded = LANES // groups
    out_rows = along_track_look_radius.shape[0]
    out_cols = range_look_radius.shape[0]
    strip_rows = out_rows * 8
    chunks = columns // LANES
    me = lax.axis_index("acq").astype(jnp.int32).reshape(1)

    squared = cell_track_displacement[0].astype(F32) ** 2
    phase = squared[..., None] * along_track_chirp_slope
    cosine, sine = jnp.cos(phase), jnp.sin(phase)
    sent = deramp(raw_echo_values, cosine, sine, [0], cell_target_line[0])
    sent += deramp(raw_echo_values, cosine, sine, list(range(1, chunks)))

    inner = jnp.arange(16, dtype=jnp.int32)
    row_mask = jnp.abs(inner - 8)[None, :] <= along_track_look_radius[:, None]
    column = 8 * jnp.arange(out_cols, dtype=jnp.int32)[:, None] - 4 + inner[None, :]
    col_mask = jnp.abs(inner - 8)[None, :] <= range_look_radius[:, None]
    col_mask = col_mask & (column >= 0) & (column < columns)
    col_mask = jnp.pad(col_mask, ((1, 0), (0, 0)))
    mask = (row_mask[:, None, :, None] & col_mask[None, :, None, :]).astype(F32)
    mask = mask.reshape(out_rows, out_cols + 1, 256)
    cmask = jnp.broadcast_to(col_mask.astype(F32)[:, :, None], (out_cols + 1, 16, LANES))

    received = []

    def receive(k, *others):
        piece = after(sent[k], *others) if others else sent[k]
        received.append(
            lax.all_to_all(piece, "strip", split_axis=0, concat_axis=0, tiled=True)
        )

    def spread(halo):
        return [halo] + [exchange(halo, "acq", bit) for bit in range(1, groups)]

    receive(0)
    receive(1, received[0])
    edge = sums = None
    waiting = None
    previous = (None, None)
    for k in range(chunks):
        final = k == chunks - 1
        own, top, bottom = make_tile(received[0], received[k], acqs, padded, strip_rows)
        if waiting is not None:
            halos = spread(previous[1])
            own = after(own, *halos)
            sums, edge = pair_sums(*waiting[:5], halos, *waiting[5:], edge, sums)
        if final:
            halo = neighbours(top, bottom)
            blocks, sources = gathered(own, padded)
        else:
            blocks, sources = gathered(own, padded)
            halo = neighbours(after(top, *blocks), after(bottom, *blocks))
        if k + 2 < chunks:
            receive(k + 2, received[k + 1], halo)
        waiting = (
            k,
            final,
            along_track_look_radius,
            mask,
            cmask,
            blocks,
            sources,
            *previous,
        )
        previous = (own, halo)
    sums, edge = pair_sums(*waiting[:5], spread(previous[1]), *waiting[5:], edge, sums)
    return finish(me, sums, acqs, groups)


def solution(mesh):
    placed = (
        P("strip", None, None, "acq", None, None),
        P("strip", None, None),
        P("strip", None, None),
        P("acq"),
        P("strip"),
        P(),
    )
    return jax.shard_map(
        per_device,
        mesh=mesh,
        in_specs=placed,
        out_specs=P("acq", None, None, "strip"),
        check_vma=False,
    )
```

time: 1450 us -> 358 us (0.25)
  matrix products: 710 us -> 0 us
  waiting for transfers between devices: 472 us -> 154 us
  Pallas kernels: 0 us -> 123 us
  local copies, waits for them, and re-layouts: 119 us -> 7.03 us
  other arithmetic: 99.9 us -> 3.41 us
  starting transfers between devices: 12.2 us -> 67.9 us
    dot_general x5 -> x0, matrix products: 710 us -> none  [the longest x4 708 us: look(): jnp.einsum('...c,cq->...q', values, colmask, precision=lax.Precision.HIGH...]
    all_to_all x2 -> x4, waiting for transfers between devices: 341 us -> 35.4 us  [receive(): lax.all_to_all(piece, 'strip', split_axis=0, concat_axis=0, tiled=True)]
    all_gather x1 -> x0, waiting for transfers between devices: 129 us -> none  [per_device(): lax.all_gather(padded, 'acq', axis=0, tiled=True)]
    pallas_call x0 -> x11, Pallas kernels: none -> 123 us  [the longest x4 69.4 us: pair_sums(): pl.pallas_call(functools.partial(pairs_kernel, k, last, sources, padded),...]
    ppermute x2 -> x36, waiting for transfers between devices: 1.88 us -> 118 us  [the longest x28 105 us: exchange(): return lax.ppermute(value, axis, [(i, i ^ bit) for i in range(size)])]
    ppermute x2 -> x36, starting transfers between devices: 3.06 us -> 45.2 us  [the longest x28 32.9 us: exchange(): return lax.ppermute(value, axis, [(i, i ^ bit) for i in range(size)])]
    reshape x5 -> x0, local copies, waits for them, and re-layouts: 42 us -> none  [the longest x3 26.9 us: windows_of(): upper = padded[:, :, :inner].reshape(acq_count, 2, inner // 8, 8, columns)]
    convert_element_type x5 -> x2, other arithmetic: 37 us -> 0.93 us  [the longest x1 0.85 us: per_device(): mask = (row_mask[:, None, :, None] & col_mask[None, :, None, :]).astype(F32)]
  transfers between devices with their start and end apart: 5 -> 40, of which waited for: 3 -> 16; matrix products, arithmetic and copies ran while one was open for 4% -> 1% of each run, Pallas kernels for 0% -> 23%
where the time goes in v1:
time: 358 us; the launch traced here: 356 us
  waiting for transfers between devices  154 us (43%)
  Pallas kernels  123 us (34%)
  starting transfers between devices  67.9 us (19%)
  local copies, waits for them, and re-layouts  7.03 us (2%)
    ppermute x28, waiting for transfers between devices, exchange(): return lax.ppermute(value, axis, [(i, i ^ bit) for i in range(size)])  105 us
    pallas_call x4, Pallas kernels, pair_sums(): pl.pallas_call(functools.partial(pairs_kernel, k, last, sources, padded),...  69.4 us
    all_to_all x4, waiting for transfers between devices, receive(): lax.all_to_all(piece, 'strip', split_axis=0, concat_axis=0, tiled=True)  35.4 us
    ppermute x28, starting transfers between devices, exchange(): return lax.ppermute(value, axis, [(i, i ^ bit) for i in range(size)])  32.9 us
    all_to_all x4, starting transfers between devices, receive(): lax.all_to_all(piece, 'strip', split_axis=0, concat_axis=0, tiled=True)  22.6 us
    pallas_call x2, Pallas kernels, deramp(): pl.pallas_call(functools.partial(deramp_kernel, acqs, chosen, lines is no...  21.1 us
    pallas_call x4, Pallas kernels, make_tile(): pl.pallas_call(functools.partial(tile_kernel, acqs, padded), grid=(1,), i...  17.9 us
    pallas_call x1, Pallas kernels, finish(): pl.pallas_call(functools.partial(finish_kernel, acqs, padded, groups), gr...  14.7 us
  transfers between devices with their start and end apart: 40, of which 16 were waited for; matrix products, arithmetic and copies ran while one was open for 1% of the time, Pallas kernels for 23%

profile of v1, /device:TPU:0, one launch (start us, length us, event | category | flops | bytes accessed | tf_op | source)
XLA Modules:
  0.0 355.8 jit_solution(4340990982192859151)
XLA Ops:
  0.7 1.6 multiply_sine_fusion
  2.3 9.5 %deramp0.1 = bf16[8,61,16,128]{3,2,1,0:T(8,128)(2,1)} custom-call(f32[30720,128]{1,0:T(8,128)} %bitcast.16, f32[8,16,30]{2,1,0:T(8,128)} %get-tuple-element.72.refs_1_, f32[8,16,30]{2,1,0:T(8,128)} %get-tuple-element.71.refs_2_, s32[8,16]{1,0:T(8,128)} %bitcast.18), custom_call_target="tpu_custom_call" | custom-call | flops 6000000000 | bytes 6000000 | tf_op jit(solution)/shard_map/deramp0/pallas_call | solution.py:100
  11.8 6.3 %all-to-all-start = ((bf16[8,61,16,128]{3,2,1,0:T(8,128)(2,1)}), bf16[8,61,16,128]{3,2,1,0:T(8,128)(2,1)S(1)}, u32[]{:S(2)}, u32[]{:S(2)}) async-start(bf16[8,61,16,128]{3,2,1,0:T(8,128)(2,1)} %deramp0.1), calls=%async_computation | async-start | bytes 3997696 | tf_op jit(solution)/shard_map/all_to_all | solution.py:555
  18.1 11.6 %deramp1.1 = (bf16[8,60,16,128]{3,2,1,0:T(8,128)(2,1)}, bf16[8,60,16,128]{3,2,1,0:T(8,128)(2,1)}, bf16[8,60,16,128]{3,2,1,0:T(8,128)(2,1)}) custom-call(f32[30720,128]{1,0:T(8,128)} %bitcast.17, f32[8,16,30]{2,1,0:T(8,128)} %get-tuple-element.72.refs_1_, f32[8,16,30]{2,1,0:T(8,128)} %get-tuple-element.71.refs_2_), custom_call_target="tpu_custom_call" | custom-call | flops 8999999488 | bytes 9000000 | tf_op jit(solution)/shard_map/deramp1/pallas_call | solution.py:100
  29.8 35.4 %all-to-all-done.lines_ref.data_ref = bf16[8,61,16,128]{3,2,1,0:T(8,128)(2,1)S(1)} async-done(((bf16[8,61,16,128]{3,2,1,0:T(8,128)(2,1)}), bf16[8,61,16,128]{3,2,1,0:T(8,128)(2,1)S(1)}, u32[]{:S(2)}, u32[]{:S(2)}) %all-to-all-start) | async-done | bytes 1998880 | tf_op jit(solution)/shard_map/all_to_all | solution.py:555
  66.4 4.4 %all-to-all-start.1 = ((bf16[8,60,16,128]{3,2,1,0:T(8,128)(2,1)}), bf16[8,60,16,128]{3,2,1,0:T(8,128)(2,1)}, u32[]{:S(2)}, u32[]{:S(2)}) async-start(bf16[8,60,16,128]{3,2,1,0:T(8,128)(2,1)} %get-tuple-element.41), calls=%async_computation.1 | async-start | bytes 3932160 | tf_op jit(solution)/shard_map/all_to_all | solution.py:555
  70.8 4.6 %tile.4 = (bf16[64,64,128]{2,1,0:T(8,128)(2,1)}, bf16[4,64,128]{2,1,0:T(8,128)(2,1)}, bf16[4,64,128]{2,1,0:T(8,128)(2,1)}) custom-call(bf16[8,61,16,128]{3,2,1,0:T(8,128)(2,1)} %copy-done, bf16[8,61,16,128]{3,2,1,0:T(8,128)(2,1)} %copy-done), custom_call_target="tpu_custom_call" | custom-call | flops 4000000000 | bytes 4000000 | tf_op jit(solution)/shard_map/tile/pallas_call | solution.py:153
  78.3 22.6 %collective-permute-done.1.refs_11_.refs_12_ = bf16[64,64,128]{2,1,0:T(8,128)(2,1)S(1)} collective-permute-done((bf16[64,64,128]{2,1,0:T(8,128)(2,1)}, bf16[64,64,128]{2,1,0:T(8,128)(2,1)S(1)}, u32[]{:S(2)}, u32[]{:S(2)}) %collective-permute-start.1) | collective-permute-done | bytes 1048608 | tf_op jit(solution)/shard_map/ppermute | solution.py:487
  102.6 1.6 collective-permute-start.3
  104.2 10.4 %collective-permute-done.2.refs_13_.refs_14_ = bf16[64,32,128]{2,1,0:T(8,128)(2,1)S(1)} collective-permute-done((bf16[64,32,128]{2,1,0:T(8,128)(2,1)S(1)}, bf16[64,32,128]{2,1,0:T(8,128)(2,1)S(1)}, u32[]{:S(2)}, u32[]{:S(2)}) %collective-permute-start.2) | collective-permute-done | bytes 524320 | tf_op jit(solution)/shard_map/ppermute | solution.py:487
  118.5 3.5 collective-permute-done.5
  122.1 6.1 %all-to-all-start.2 = ((bf16[8,60,16,128]{3,2,1,0:T(8,128)(2,1)}), bf16[8,60,16,128]{3,2,1,0:T(8,128)(2,1)S(1)}, u32[]{:S(2)}, u32[]{:S(2)}) async-start(bf16[8,60,16,128]{3,2,1,0:T(8,128)(2,1)} %get-tuple-element.47), calls=%async_computation.2 | async-start | bytes 3932160 | tf_op jit(solution)/shard_map/all_to_all | solution.py:555
  131.7 4.5 %tile.5 = (bf16[64,64,128]{2,1,0:T(8,128)(2,1)}, bf16[4,64,128]{2,1,0:T(8,128)(2,1)}, bf16[4,64,128]{2,1,0:T(8,128)(2,1)}) custom-call(bf16[8,61,16,128]{3,2,1,0:T(8,128)(2,1)} %copy-done, bf16[8,60,16,128]{3,2,1,0:T(8,128)(2,1)} %all-to-all-done.1.data_ref), custom_call_target="tpu_custom_call" | custom-call | flops 4000000000 | bytes 4000000 | tf_op jit(solution)/shard_map/tile/pallas_call | solution.py:153
  140.2 22.6 %collective-permute-done.10.refs_11_.refs_12_ = bf16[64,64,128]{2,1,0:T(8,128)(2,1)S(1)} collective-permute-done((bf16[64,64,128]{2,1,0:T(8,128)(2,1)}, bf16[64,64,128]{2,1,0:T(8,128)(2,1)S(1)}, u32[]{:S(2)}, u32[]{:S(2)}) %collective-permute-start.10) | collective-permute-done | bytes 1048608 | tf_op jit(solution)/shard_map/ppermute | solution.py:487
  165.1 10.5 %collective-permute-done.11.refs_13_.refs_14_ = bf16[64,32,128]{2,1,0:T(8,128)(2,1)S(1)} collective-permute-done((bf16[64,32,128]{2,1,0:T(8,128)(2,1)S(1)}, bf16[64,32,128]{2,1,0:T(8,128)(2,1)S(1)}, u32[]{:S(2)}, u32[]{:S(2)}) %collective-permute-start.11) | collective-permute-done | bytes 524320 | tf_op jit(solution)/shard_map/ppermute | solution.py:487
  179.2 3.0 collective-permute-done.14
  183.9 2.1 collective-permute-start.22
  187.2 5.9 %all-to-all-start.3 = ((bf16[8,60,16,128]{3,2,1,0:T(8,128)(2,1)}), bf16[8,60,16,128]{3,2,1,0:T(8,128)(2,1)S(1)}, u32[]{:S(2)}, u32[]{:S(2)}) async-start(bf16[8,60,16,128]{3,2,1,0:T(8,128)(2,1)} %get-tuple-element.54), calls=%async_computation.3 | async-start | bytes 3932160 | tf_op jit(solution)/shard_map/all_to_all | solution.py:555
  193.1 4.4 %tile.7 = (bf16[64,64,128]{2,1,0:T(8,128)(2,1)}, bf16[4,64,128]{2,1,0:T(8,128)(2,1)}, bf16[4,64,128]{2,1,0:T(8,128)(2,1)}) custom-call(bf16[8,61,16,128]{3,2,1,0:T(8,128)(2,1)} %copy-done, bf16[8,60,16,128]{3,2,1,0:T(8,128)(2,1)} %copy-done.2), custom_call_target="tpu_custom_call" | custom-call | flops 4000000000 | bytes 4000000 | tf_op jit(solution)/shard_map/tile/pallas_call | solution.py:153
  199.2 24.2 %collective-permute-done.24.refs_11_.refs_12_ = bf16[64,64,128]{2,1,0:T(8,128)(2,1)S(1)} collective-permute-done((bf16[64,64,128]{2,1,0:T(8,128)(2,1)}, bf16[64,64,128]{2,1,0:T(8,128)(2,1)S(1)}, u32[]{:S(2)}, u32[]{:S(2)}) %collective-permute-start.24) | collective-permute-done | bytes 1048608 | tf_op jit(solution)/shard_map/ppermute | solution.py:487
  227.0 10.2 %collective-permute-done.25.refs_13_.refs_14_ = bf16[64,32,128]{2,1,0:T(8,128)(2,1)} collective-permute-done((bf16[64,32,128]{2,1,0:T(8,128)(2,1)S(1)}, bf16[64,32,128]{2,1,0:T(8,128)(2,1)}, u32[]{:S(2)}, u32[]{:S(2)}) %collective-permute-start.25) | collective-permute-done | bytes 524320 | tf_op jit(solution)/shard_map/ppermute | solution.py:487
  240.3 16.4 %pairs0.1 = (f32[8,64,64,128]{3,2,1,0:T(8,128)}, f32[72,16,256]{2,1,0:T(8,128)}) custom-call(s32[8]{0:T(128)} %refs_0_.7, f32[8,65,256]{2,1,0:T(8,128)} %and_convert_fusion.refs_1_, f32[65,16,128]{2,1,0:T(8,128)} %broadcast_in_dim.2.refs_2_, bf16[8,64,128]{2,1,0:T(8,128)(2,1)} %copy-done.11, bf16[8,64,128]{2,1,0:T(8,128)(2,1)} %copy-done.23, ...), custom_call_target="tpu_custom_call" | custom-call | flops 16000000000 | bytes 16000000 | tf_op jit(solution)/shard_map/pairs0/pallas_call | solution.py:401
  258.2 3.1 collective-permute-done.28
  263.0 1.9 collective-permute-start.31
  266.2 4.5 %tile.6 = (bf16[64,64,128]{2,1,0:T(8,128)(2,1)}, bf16[4,64,128]{2,1,0:T(8,128)(2,1)}, bf16[4,64,128]{2,1,0:T(8,128)(2,1)}) custom-call(bf16[8,61,16,128]{3,2,1,0:T(8,128)(2,1)} %copy-done, bf16[8,60,16,128]{3,2,1,0:T(8,128)(2,1)} %copy-done.1), custom_call_target="tpu_custom_call" | custom-call | flops 4000000000 | bytes 4000000 | tf_op jit(solution)/shard_map/tile/pallas_call | solution.py:153
  272.7 3.1 collective-permute-start.15
  275.8 17.9 %pairs1.1 = (f32[8,64,64,128]{3,2,1,0:T(8,128)}, f32[72,16,256]{2,1,0:T(8,128)}) custom-call(s32[8]{0:T(128)} %refs_0_.7, f32[8,65,256]{2,1,0:T(8,128)} %and_convert_fusion.refs_1_, f32[65,16,128]{2,1,0:T(8,128)} %broadcast_in_dim.2.refs_2_, bf16[8,64,128]{2,1,0:T(8,128)(2,1)} %copy-done.12, ...), custom_call_target="tpu_custom_call", output_to_operand_aliasing={{0}: (21, {})} | custom-call | flops 16000000000 | bytes 16000000 | tf_op jit(solution)/shard_map/pairs1/pallas_call | solution.py:401
  295.1 3.2 collective-permute-done.16
  303.1 1.6 collective-permute-start.35
  304.7 17.9 %pairs2.1 = (f32[8,64,64,128]{3,2,1,0:T(8,128)}, f32[72,16,256]{2,1,0:T(8,128)}) custom-call(s32[8]{0:T(128)} %refs_0_.7, f32[8,65,256]{2,1,0:T(8,128)} %and_convert_fusion.refs_1_, f32[65,16,128]{2,1,0:T(8,128)} %broadcast_in_dim.2.refs_2_, bf16[8,64,128]{2,1,0:T(8,128)(2,1)} %copy-done.13, ...), custom_call_target="tpu_custom_call", output_to_operand_aliasing={{0}: (21, {})} | custom-call | flops 16000000000 | bytes 16000000 | tf_op jit(solution)/shard_map/pairs2/pallas_call | solution.py:401
  323.8 17.3 %pairs3.1.real_ref.imag_ref.energy_ref = f32[8,64,64,128]{3,2,1,0:T(8,128)} custom-call(s32[8]{0:T(128)} %refs_0_.7, f32[8,65,256]{2,1,0:T(8,128)} %and_convert_fusion.refs_1_, f32[65,16,128]{2,1,0:T(8,128)} %broadcast_in_dim.2.refs_2_, bf16[8,64,128]{2,1,0:T(8,128)(2,1)} %copy-done.14, ...), custom_call_target="tpu_custom_call", output_to_operand_aliasing={{}: (21, {})} | custom-call | flops 16000000000 | bytes 16000000 | tf_op jit(solution)/shard_map/pairs3/pallas_call | solution.py:401
  341.1 14.7 %finish.1 = f32[30,960,128]{2,1,0:T(8,128)} custom-call(s32[1]{0:T(128)} %bitcast.me_ref, f32[8,64,64,128]{3,2,1,0:T(8,128)} %pairs3.1.real_ref.imag_ref.energy_ref, f32[8,64,64,128]{3,2,1,0:T(8,128)} %pairs3.1.real_ref.imag_ref.energy_ref, f32[8,64,64,128]{3,2,1,0:T(8,128)} %pairs3.1.real_ref.imag_ref.energy_ref), custom_call_target="tpu_custom_call" | custom-call | flops 25165824 | bytes 33554432 | tf_op jit(solution)/shard_map/finish/pallas_call | solution.py:463
  (173 shorter events, 48.7 us)
Async XLA Ops:
  11.8 53.3 %all-to-all-start = ((bf16[8,61,16,128]{3,2,1,0:T(8,128)(2,1)}), bf16[8,61,16,128]{3,2,1,0:T(8,128)(2,1)S(1)}, u32[]{:S(2)}, u32[]{:S(2)}) async-start(bf16[8,61,16,128]{3,2,1,0:T(8,128)(2,1)} %deramp0.1), calls=%async_computation | async-start | bytes 3997696 | tf_op jit(solution)/shard_map/all_to_all | solution.py:555
  66.4 55.7 %all-to-all-start.1 = ((bf16[8,60,16,128]{3,2,1,0:T(8,128)(2,1)}), bf16[8,60,16,128]{3,2,1,0:T(8,128)(2,1)}, u32[]{:S(2)}, u32[]{:S(2)}) async-start(bf16[8,60,16,128]{3,2,1,0:T(8,128)(2,1)} %get-tuple-element.41), calls=%async_computation.1 | async-start | bytes 3932160 | tf_op jit(solution)/shard_map/all_to_all | solution.py:555
  75.3 25.6 %collective-permute-start.1 = (bf16[64,64,128]{2,1,0:T(8,128)(2,1)}, bf16[64,64,128]{2,1,0:T(8,128)(2,1)S(1)}, u32[]{:S(2)}, u32[]{:S(2)}) collective-permute-start(bf16[64,64,128]{2,1,0:T(8,128)(2,1)} %get-tuple-element.43.refs_7_.refs_8_.refs_17_.refs_18_), channel_id=1, source_target_pairs={{0,16},{8,24},{16,0},{24,8},{1,17},{9,25},{17,1},{25,9},{2,18},{10... | collective-permute-start | bytes 3145736 | tf_op jit(solution)/shard_map/ppermute | solution.py:487
  76.9 25.7 %collective-permute-start = (bf16[64,64,128]{2,1,0:T(8,128)(2,1)}, bf16[64,64,128]{2,1,0:T(8,128)(2,1)S(1)}, u32[]{:S(2)}, u32[]{:S(2)}) collective-permute-start(bf16[64,64,128]{2,1,0:T(8,128)(2,1)} %get-tuple-element.43.refs_7_.refs_8_.refs_17_.refs_18_), channel_id=1, source_target_pairs={{0,8},{8,0},{16,24},{24,16},{1,9},{9,1},{17,25},{25,17},{2,10},{10... | collective-permute-start | bytes 3145736 | tf_op jit(solution)/shard_map/ppermute | solution.py:487
  101.0 13.5 %collective-permute-start.2 = (bf16[64,32,128]{2,1,0:T(8,128)(2,1)S(1)}, bf16[64,32,128]{2,1,0:T(8,128)(2,1)S(1)}, u32[]{:S(2)}, u32[]{:S(2)}) collective-permute-start(bf16[64,32,128]{2,1,0:T(8,128)(2,1)S(1)} %slice.32), channel_id=1, source_target_pairs={{0,8},{8,0},{16,24},{24,16},{1,9},{9,1},{17,25},{25,17},{2,10},{10... | collective-permute-start | bytes 1572872 | tf_op jit(solution)/shard_map/ppermute | solution.py:487
  102.6 13.3 %collective-permute-start.3 = (bf16[64,32,128]{2,1,0:T(8,128)(2,1)S(1)}, bf16[64,32,128]{2,1,0:T(8,128)(2,1)S(1)}, u32[]{:S(2)}, u32[]{:S(2)}) collective-permute-start(bf16[64,32,128]{2,1,0:T(8,128)(2,1)S(1)} %slice.33), channel_id=1, source_target_pairs={{0,16},{8,24},{16,0},{24,8},{1,17},{9,25},{17,1},{25,9},{2,18},{10... | collective-permute-start | bytes 1572872 | tf_op jit(solution)/shard_map/ppermute | solution.py:487
  122.1 63.9 %all-to-all-start.2 = ((bf16[8,60,16,128]{3,2,1,0:T(8,128)(2,1)}), bf16[8,60,16,128]{3,2,1,0:T(8,128)(2,1)S(1)}, u32[]{:S(2)}, u32[]{:S(2)}) async-start(bf16[8,60,16,128]{3,2,1,0:T(8,128)(2,1)} %get-tuple-element.47), calls=%async_computation.2 | async-start | bytes 3932160 | tf_op jit(solution)/shard_map/all_to_all | solution.py:555
  128.2 8.0 %collective-permute-start.6 = (bf16[8,64,128]{2,1,0:T(8,128)(2,1)S(1)}, bf16[8,64,128]{2,1,0:T(8,128)(2,1)S(1)}, u32[]{:S(2)}, u32[]{:S(2)}) collective-permute-start(bf16[8,64,128]{2,1,0:T(8,128)(2,1)S(1)} %constant_dynamic-update-slice_fusion.refs_3_.refs_19_), channel_id=1, source_target_pairs={{0,8},{8,0},{16,24},{24,16},{1,9},{9,1},{17,25},{25,17},{2,10},{10... | collective-permute-start | bytes 393224 | tf_op jit(solution)/shard_map/ppermute | solution.py:487
  137.8 25.0 %collective-permute-start.10 = (bf16[64,64,128]{2,1,0:T(8,128)(2,1)}, bf16[64,64,128]{2,1,0:T(8,128)(2,1)S(1)}, u32[]{:S(2)}, u32[]{:S(2)}) collective-permute-start(bf16[64,64,128]{2,1,0:T(8,128)(2,1)} %get-tuple-element.50.refs_7_.refs_8_.refs_17_.refs_18_), channel_id=1, source_target_pairs={{0,16},{8,24},{16,0},{24,8},{1,17},{9,25},{17,1},{25,9},{2,18},{10... | collective-permute-start | bytes 3145736 | tf_op jit(solution)/shard_map/ppermute | solution.py:487
  139.4 24.8 %collective-permute-start.9 = (bf16[64,64,128]{2,1,0:T(8,128)(2,1)}, bf16[64,64,128]{2,1,0:T(8,128)(2,1)S(1)}, u32[]{:S(2)}, u32[]{:S(2)}) collective-permute-start(bf16[64,64,128]{2,1,0:T(8,128)(2,1)} %get-tuple-element.50.refs_7_.refs_8_.refs_17_.refs_18_), channel_id=1, source_target_pairs={{0,8},{8,0},{16,24},{24,16},{1,9},{9,1},{17,25},{25,17},{2,10},{10... | collective-permute-start | bytes 3145736 | tf_op jit(solution)/shard_map/ppermute | solution.py:487
  162.9 12.7 %collective-permute-start.11 = (bf16[64,32,128]{2,1,0:T(8,128)(2,1)S(1)}, bf16[64,32,128]{2,1,0:T(8,128)(2,1)S(1)}, u32[]{:S(2)}, u32[]{:S(2)}) collective-permute-start(bf16[64,32,128]{2,1,0:T(8,128)(2,1)S(1)} %slice.34), channel_id=1, source_target_pairs={{0,8},{8,0},{16,24},{24,16},{1,9},{9,1},{17,25},{25,17},{2,10},{10... | collective-permute-start | bytes 1572872 | tf_op jit(solution)/shard_map/ppermute | solution.py:487
  164.2 12.5 %collective-permute-start.12 = (bf16[64,32,128]{2,1,0:T(8,128)(2,1)S(1)}, bf16[64,32,128]{2,1,0:T(8,128)(2,1)S(1)}, u32[]{:S(2)}, u32[]{:S(2)}) collective-permute-start(bf16[64,32,128]{2,1,0:T(8,128)(2,1)S(1)} %slice.35), channel_id=1, source_target_pairs={{0,16},{8,24},{16,0},{24,8},{1,17},{9,25},{17,1},{25,9},{2,18},{10... | collective-permute-start | bytes 1572872 | tf_op jit(solution)/shard_map/ppermute | solution.py:487
  182.3 15.2 %collective-permute-start.20 = (bf16[8,64,128]{2,1,0:T(8,128)(2,1)S(1)}, bf16[8,64,128]{2,1,0:T(8,128)(2,1)S(1)}, u32[]{:S(2)}, u32[]{:S(2)}) collective-permute-start(bf16[8,64,128]{2,1,0:T(8,128)(2,1)S(1)} %constant_dynamic-update-slice_fusion.2.refs_3_.refs_19_), channel_id=1, source_target_pairs={{0,8},{8,0},{16,24},{24,16},{1,9},{9,1},{17,25},{25,17},{2,10},{10... | collective-permute-start | bytes 393224 | tf_op jit(solution)/shard_map/ppermute | solution.py:487
  183.4 14.2 %collective-permute-start.21 = (bf16[8,64,128]{2,1,0:T(8,128)(2,1)S(1)}, bf16[8,64,128]{2,1,0:T(8,128)(2,1)S(1)}, u32[]{:S(2)}, u32[]{:S(2)}) collective-permute-start(bf16[8,64,128]{2,1,0:T(8,128)(2,1)S(1)} %constant_dynamic-update-slice_fusion.2.refs_3_.refs_19_), channel_id=1, source_target_pairs={{0,16},{8,24},{16,0},{24,8},{1,17},{9,25},{17,1},{25,9},{2,18},{10... | collective-permute-start | bytes 393224 | tf_op jit(solution)/shard_map/ppermute | solution.py:487
  183.9 13.7 %collective-permute-start.22 = (bf16[8,64,128]{2,1,0:T(8,128)(2,1)S(1)}, bf16[8,64,128]{2,1,0:T(8,128)(2,1)S(1)}, u32[]{:S(2)}, u32[]{:S(2)}) collective-permute-start(bf16[8,64,128]{2,1,0:T(8,128)(2,1)S(1)} %constant_dynamic-update-slice_fusion.2.refs_3_.refs_19_), channel_id=1, source_target_pairs={{0,24},{8,16},{16,8},{24,0},{1,25},{9,17},{17,9},{25,1},{2,26},{10... | collective-permute-start | bytes 393224 | tf_op jit(solution)/shard_map/ppermute | solution.py:487
  187.2 77.7 %all-to-all-start.3 = ((bf16[8,60,16,128]{3,2,1,0:T(8,128)(2,1)}), bf16[8,60,16,128]{3,2,1,0:T(8,128)(2,1)S(1)}, u32[]{:S(2)}, u32[]{:S(2)}) async-start(bf16[8,60,16,128]{3,2,1,0:T(8,128)(2,1)} %get-tuple-element.54), calls=%async_computation.3 | async-start | bytes 3932160 | tf_op jit(solution)/shard_map/all_to_all | solution.py:555
  197.6 25.8 %collective-permute-start.24 = (bf16[64,64,128]{2,1,0:T(8,128)(2,1)}, bf16[64,64,128]{2,1,0:T(8,128)(2,1)S(1)}, u32[]{:S(2)}, u32[]{:S(2)}) collective-permute-start(bf16[64,64,128]{2,1,0:T(8,128)(2,1)} %get-tuple-element.60.refs_7_.refs_8_.refs_17_.refs_18_), channel_id=1, source_target_pairs={{0,16},{8,24},{16,0},{24,8},{1,17},{9,25},{17,1},{25,9},{2,18},{10... | collective-permute-start | bytes 3145736 | tf_op jit(solution)/shard_map/ppermute | solution.py:487
  198.1 26.4 %collective-permute-start.23 = (bf16[64,64,128]{2,1,0:T(8,128)(2,1)}, bf16[64,64,128]{2,1,0:T(8,128)(2,1)S(1)}, u32[]{:S(2)}, u32[]{:S(2)}) collective-permute-start(bf16[64,64,128]{2,1,0:T(8,128)(2,1)} %get-tuple-element.60.refs_7_.refs_8_.refs_17_.refs_18_), channel_id=1, source_target_pairs={{0,8},{8,0},{16,24},{24,16},{1,9},{9,1},{17,25},{25,17},{2,10},{10... | collective-permute-start | bytes 3145736 | tf_op jit(solution)/shard_map/ppermute | solution.py:487
  223.5 13.7 %collective-permute-start.25 = (bf16[64,32,128]{2,1,0:T(8,128)(2,1)S(1)}, bf16[64,32,128]{2,1,0:T(8,128)(2,1)}, u32[]{:S(2)}, u32[]{:S(2)}) collective-permute-start(bf16[64,32,128]{2,1,0:T(8,128)(2,1)S(1)} %slice.36), channel_id=1, source_target_pairs={{0,8},{8,0},{16,24},{24,16},{1,9},{9,1},{17,25},{25,17},{2,10},{10... | collective-permute-start | bytes 1572872 | tf_op jit(solution)/shard_map/ppermute | solution.py:487
  224.6 13.4 %collective-permute-start.26 = (bf16[64,32,128]{2,1,0:T(8,128)(2,1)S(1)}, bf16[64,32,128]{2,1,0:T(8,128)(2,1)}, u32[]{:S(2)}, u32[]{:S(2)}) collective-permute-start(bf16[64,32,128]{2,1,0:T(8,128)(2,1)S(1)} %slice.37), channel_id=1, source_target_pairs={{0,16},{8,24},{16,0},{24,8},{1,17},{9,25},{17,1},{25,9},{2,18},{10... | collective-permute-start | bytes 1572872 | tf_op jit(solution)/shard_map/ppermute | solution.py:487
  238.0 20.2 %collective-permute-start.27 = (bf16[4,64,128]{2,1,0:T(8,128)(2,1)S(1)}, bf16[4,64,128]{2,1,0:T(8,128)(2,1)S(1)}, u32[]{:S(2)}, u32[]{:S(2)}) collective-permute-start(bf16[4,64,128]{2,1,0:T(8,128)(2,1)S(1)} %copy-done.36), channel_id=1, source_target_pairs={{0,1},{1,2},{2,3},{3,4},{4,5},{5,6},{6,7},{8,9},{9,10},{10,11},{11... | collective-permute-start | bytes 196616 | tf_op jit(solution)/shard_map/ppermute | solution.py:494
  261.4 9.3 %collective-permute-start.29 = (bf16[8,64,128]{2,1,0:T(8,128)(2,1)S(1)}, bf16[8,64,128]{2,1,0:T(8,128)(2,1)S(1)}, u32[]{:S(2)}, u32[]{:S(2)}) collective-permute-start(bf16[8,64,128]{2,1,0:T(8,128)(2,1)S(1)} %constant_dynamic-update-slice_fusion.6.refs_3_.refs_19_), channel_id=1, source_target_pairs={{0,8},{8,0},{16,24},{24,16},{1,9},{9,1},{17,25},{25,17},{2,10},{10... | collective-permute-start | bytes 393224 | tf_op jit(solution)/shard_map/ppermute | solution.py:487
  262.5 8.2 %collective-permute-start.30 = (bf16[8,64,128]{2,1,0:T(8,128)(2,1)S(1)}, bf16[8,64,128]{2,1,0:T(8,128)(2,1)S(1)}, u32[]{:S(2)}, u32[]{:S(2)}) collective-permute-start(bf16[8,64,128]{2,1,0:T(8,128)(2,1)S(1)} %constant_dynamic-update-slice_fusion.6.refs_3_.refs_19_), channel_id=1, source_target_pairs={{0,16},{8,24},{16,0},{24,8},{1,17},{9,25},{17,1},{25,9},{2,18},{10... | collective-permute-start | bytes 393224 | tf_op jit(solution)/shard_map/ppermute | solution.py:487
  263.0 7.6 %collective-permute-start.31 = (bf16[8,64,128]{2,1,0:T(8,128)(2,1)S(1)}, bf16[8,64,128]{2,1,0:T(8,128)(2,1)S(1)}, u32[]{:S(2)}, u32[]{:S(2)}) collective-permute-start(bf16[8,64,128]{2,1,0:T(8,128)(2,1)S(1)} %constant_dynamic-update-slice_fusion.6.refs_3_.refs_19_), channel_id=1, source_target_pairs={{0,24},{8,16},{16,8},{24,0},{1,25},{9,17},{17,9},{25,1},{2,26},{10... | collective-permute-start | bytes 393224 | tf_op jit(solution)/shard_map/ppermute | solution.py:487
  270.7 31.2 %collective-permute-start.33 = (bf16[64,64,128]{2,1,0:T(8,128)(2,1)}, bf16[64,64,128]{2,1,0:T(8,128)(2,1)S(1)}, u32[]{:S(2)}, u32[]{:S(2)}) collective-permute-start(bf16[64,64,128]{2,1,0:T(8,128)(2,1)} %get-tuple-element.64.refs_7_.refs_8_), channel_id=1, source_target_pairs={{0,16},{8,24},{16,0},{24,8},{1,17},{9,25},{17,1},{25,9},{2,18},{10... | collective-permute-start | bytes 3145736 | tf_op jit(solution)/shard_map/ppermute | solution.py:487
  271.7 31.3 %collective-permute-start.32 = (bf16[64,64,128]{2,1,0:T(8,128)(2,1)}, bf16[64,64,128]{2,1,0:T(8,128)(2,1)S(1)}, u32[]{:S(2)}, u32[]{:S(2)}) collective-permute-start(bf16[64,64,128]{2,1,0:T(8,128)(2,1)} %get-tuple-element.64.refs_7_.refs_8_), channel_id=1, source_target_pairs={{0,8},{8,0},{16,24},{24,16},{1,9},{9,1},{17,25},{25,17},{2,10},{10... | collective-permute-start | bytes 3145736 | tf_op jit(solution)/shard_map/ppermute | solution.py:487
  272.7 22.4 %collective-permute-start.15 = (bf16[4,64,128]{2,1,0:T(8,128)(2,1)}, bf16[4,64,128]{2,1,0:T(8,128)(2,1)S(1)}, u32[]{:S(2)}, u32[]{:S(2)}) collective-permute-start(bf16[4,64,128]{2,1,0:T(8,128)(2,1)} %get-tuple-element.55), channel_id=1, source_target_pairs={{0,1},{1,2},{2,3},{3,4},{4,5},{5,6},{6,7},{8,9},{9,10},{10,11},{11... | collective-permute-start | bytes 196616 | tf_op jit(solution)/shard_map/ppermute | solution.py:494
  298.4 24.3 %collective-permute-start.17 = (bf16[8,64,128]{2,1,0:T(8,128)(2,1)S(1)}, bf16[8,64,128]{2,1,0:T(8,128)(2,1)S(1)}, u32[]{:S(2)}, u32[]{:S(2)}) collective-permute-start(bf16[8,64,128]{2,1,0:T(8,128)(2,1)S(1)} %constant_dynamic-update-slice_fusion.4.refs_3_), channel_id=1, source_target_pairs={{0,8},{8,0},{16,24},{24,16},{1,9},{9,1},{17,25},{25,17},{2,10},{10... | collective-permute-start | bytes 393224 | tf_op jit(solution)/shard_map/ppermute | solution.py:487
  299.5 23.2 %collective-permute-start.18 = (bf16[8,64,128]{2,1,0:T(8,128)(2,1)S(1)}, bf16[8,64,128]{2,1,0:T(8,128)(2,1)S(1)}, u32[]{:S(2)}, u32[]{:S(2)}) collective-permute-start(bf16[8,64,128]{2,1,0:T(8,128)(2,1)S(1)} %constant_dynamic-update-slice_fusion.4.refs_3_), channel_id=1, source_target_pairs={{0,16},{8,24},{16,0},{24,8},{1,17},{9,25},{17,1},{25,9},{2,18},{10... | collective-permute-start | bytes 393224 | tf_op jit(solution)/shard_map/ppermute | solution.py:487
  301.0 21.7 %collective-permute-start.19 = (bf16[8,64,128]{2,1,0:T(8,128)(2,1)S(1)}, bf16[8,64,128]{2,1,0:T(8,128)(2,1)S(1)}, u32[]{:S(2)}, u32[]{:S(2)}) collective-permute-start(bf16[8,64,128]{2,1,0:T(8,128)(2,1)S(1)} %constant_dynamic-update-slice_fusion.4.refs_3_), channel_id=1, source_target_pairs={{0,24},{8,16},{16,8},{24,0},{1,25},{9,17},{17,9},{25,1},{2,26},{10... | collective-permute-start | bytes 393224 | tf_op jit(solution)/shard_map/ppermute | solution.py:487
  301.9 20.7 %collective-permute-start.34 = (bf16[64,32,128]{2,1,0:T(8,128)(2,1)S(1)}, bf16[64,32,128]{2,1,0:T(8,128)(2,1)S(1)}, u32[]{:S(2)}, u32[]{:S(2)}) collective-permute-start(bf16[64,32,128]{2,1,0:T(8,128)(2,1)S(1)} %slice.38), channel_id=1, source_target_pairs={{0,8},{8,0},{16,24},{24,16},{1,9},{9,1},{17,25},{25,17},{2,10},{10... | collective-permute-start | bytes 1572872 | tf_op jit(solution)/shard_map/ppermute | solution.py:487
  303.1 19.6 %collective-permute-start.35 = (bf16[64,32,128]{2,1,0:T(8,128)(2,1)S(1)}, bf16[64,32,128]{2,1,0:T(8,128)(2,1)S(1)}, u32[]{:S(2)}, u32[]{:S(2)}) collective-permute-start(bf16[64,32,128]{2,1,0:T(8,128)(2,1)S(1)} %slice.39), channel_id=1, source_target_pairs={{0,16},{8,24},{16,0},{24,8},{1,17},{9,25},{17,1},{25,9},{2,18},{10... | collective-permute-start | bytes 1572872 | tf_op jit(solution)/shard_map/ppermute | solution.py:487
  (50 other events, 726.0 us)

commit v2 on v1

--- a/solution.py
+++ b/solution.py
@@ -229,7 +229,7 @@
     def rows_of(low_ref, high_ref, halo, xx, size):
         main = low_ref[xx, size, :] if xx < 4 else high_ref[xx - 4, size, :]
         edge = at_top if xx < 4 else at_bottom
-        return jnp.where(edge, halo.astype(F32), main.astype(F32))
+        return jnp.where(edge, halo, main)
 
     slot_now = lax.rem(y, 2)
     slot_old = 1 - slot_now
@@ -248,7 +248,8 @@
                 for i, (index, offset) in enumerate(part)
             ]
             parts.append(jnp.concatenate(pieces, axis=0).T)
-        value = jnp.concatenate(parts, axis=1)
+        narrow = jnp.concatenate(parts, axis=1)
+        value = narrow.astype(F32)
         top = value[:8]
         bottom = value[LANES - 8 :]
         if first:
@@ -258,7 +259,8 @@
             tail = edge_ref[xx, :8]
             start = jnp.where(early, edge_ref[xx, 8:], top)
             proper = jnp.concatenate([start, value[8:]], axis=0)
-        even[x] = proper.reshape(8, 16, width).astype(BF16)
+        even[x, 0] = proper[:16].astype(BF16)
+        even[x, 1:] = narrow[16:].reshape(7, 16, width)
         shifted = jnp.concatenate([tail, proper[: LANES - 8]], axis=0)
         odd[x] = shifted.reshape(8, 16, width).astype(BF16)
         levels = [squares(tail), squares(proper)]
@@ -278,13 +280,14 @@
         power[slot_old] = power[slot_old] + old
 
     raw = [
-        rows_of(blocks[0], blocks[1], halos[0][xx], xx, slice(None)) for xx in range(8)
+        rows_of(blocks[0], blocks[1], halos[0][xx], xx, slice(None)).astype(F32)
+        for xx in range(8)
     ]
     owned = raw
     rolled = [pltpu.roll(value, 8, 1) for value in owned]
     if not first:
         before = [
-            rows_of(before[0], before[1], before_halo_ref[xx], xx, slice(None))
+            rows_of(before[0], before[1], before_halo_ref[xx], xx, slice(None)).astype(F32)
             for xx in range(8)
         ]
         owned = [jnp.where(lane < 4, before[xx], raw[xx]) for xx in range(8)]
@@ -350,7 +353,8 @@
 
 
 def pair_sums(
-    k, last, radius, mask, cmask, halos, blocks, sources, before, before_halo, edge, sums
+    k, last, radius, mask, cmask, halos, part, blocks, sources,
+    before, before_halo, part_before, edge, sums,
 ):
     strip_rows, rows2, _ = blocks[0].shape
     rows = strip_rows + 8
@@ -373,20 +377,23 @@
     def whole(array):
         return pl.BlockSpec(array.shape, lambda y: (0,) * array.ndim)
 
+    def halo_part(number):
+        return pl.BlockSpec((8, rows2, LANES), lambda y: (0, number, 0))
+
     edge_shape = jax.ShapeDtypeStruct((rows, 16, width), F32)
     args = [radius, mask, cmask, *halos]
     in_specs = [
         pl.BlockSpec(memory_space=pltpu.SMEM),
         pl.BlockSpec((1, *mask.shape[1:]), lambda y: (jnp.maximum(y - 1, 0), 0, 0)),
         whole(cmask),
-        *[whole(halo) for halo in halos],
+        *[halo_part(part) for _ in halos],
     ]
     for block in blocks:
         args += [block, block]
         in_specs += by_halves(block)
     if not first:
         args += [before, before, before_halo, edge]
-        in_specs += [*by_halves(before), whole(before_halo), by_rows(edge)]
+        in_specs += [*by_halves(before), halo_part(part_before), by_rows(edge)]
     aliases = {}
     if not first:
         args.append(sums)
@@ -555,41 +562,59 @@
             lax.all_to_all(piece, "strip", split_axis=0, concat_axis=0, tiled=True)
         )
 
-    def spread(halo):
-        return [halo] + [exchange(halo, "acq", bit) for bit in range(1, groups)]
-
+    def spread(tops, bottoms):
+        halo = neighbours(jnp.concatenate(tops, axis=1), jnp.concatenate(bottoms, axis=1))
+        return halo, lambda: [halo] + [exchange(halo, "acq", bit) for bit in range(1, groups)]
+
+    common = (along_track_look_radius, mask, cmask)
+    owns, tops, bottoms, gathers = [], [], [], []
+
+    def tile(k, *others):
+        data = after(received[k], *others) if others else received[k]
+        own, top, bottom = make_tile(received[0], data, acqs, padded, strip_rows)
+        tops.append(top)
+        bottoms.append(bottom)
+        return own
+
+    def sums_of(k, halos, part, halos_before, part_before, edge, sums):
+        before = owns[k - 1] if k else None
+        return pair_sums(
+            k, k == chunks - 1, *common, halos, part, *gathers[k],
+            before, halos_before, part_before, edge, sums,
+        )
+
+    half = chunks // 2
     receive(0)
-    receive(1, received[0])
+    for k in range(half):
+        receive(k + 1, received[k], *(gathers[k - 1][0] if k else ()))
+        owns.append(tile(k))
+        gathers.append(gathered(owns[k], padded))
+    edges, send_edges = spread(
+        [after(top, received[half]) for top in tops],
+        [after(bottom, received[half]) for bottom in bottoms],
+    )
     edge = sums = None
-    waiting = None
-    previous = (None, None)
-    for k in range(chunks):
-        final = k == chunks - 1
-        own, top, bottom = make_tile(received[0], received[k], acqs, padded, strip_rows)
-        if waiting is not None:
-            halos = spread(previous[1])
-            own = after(own, *halos)
-            sums, edge = pair_sums(*waiting[:5], halos, *waiting[5:], edge, sums)
-        if final:
-            halo = neighbours(top, bottom)
-            blocks, sources = gathered(own, padded)
-        else:
-            blocks, sources = gathered(own, padded)
-            halo = neighbours(after(top, *blocks), after(bottom, *blocks))
-        if k + 2 < chunks:
-            receive(k + 2, received[k + 1], halo)
-        waiting = (
-            k,
-            final,
-            along_track_look_radius,
-            mask,
-            cmask,
-            blocks,
-            sources,
-            *previous,
-        )
-        previous = (own, halo)
-    sums, edge = pair_sums(*waiting[:5], spread(previous[1]), *waiting[5:], edge, sums)
+    early = late = None
+    for k in range(half, chunks):
+        if k + 1 < chunks:
+            receive(k + 1, received[k], edges, *gathers[k - 1][0])
+        own = tile(k, edge, *gathers[k - 1][0]) if k > half else tile(k)
+        if early is None:
+            early = send_edges()
+        own = after(own, *early)
+        owns.append(own)
+        filler = ()
+        if k == half:
+            for i in range(half):
+                sums, edge = sums_of(i, early, i, early[0], i - 1, edge, sums)
+                if not filler:
+                    filler = (edge,)
+        gathers.append(gathered(own, padded, filler))
+    edges, send_edges = spread(tops[half:], bottoms[half:])
+    late = send_edges()
+    for k in range(half, chunks):
+        before = (early[0], half - 1) if k == half else (late[0], k - half - 1)
+        sums, edge = sums_of(k, late, k - half, *before, edge, sums)
     return finish(me, sums, acqs, groups)
 
 

time: 358 us -> 337 us (0.941)
  starting transfers between devices: 67.9 us -> 52.8 us
  waiting for transfers between devices: 154 us -> 145 us
    all_to_all x4, waiting for transfers between devices: 35.4 us -> 48.2 us  [receive(): lax.all_to_all(piece, 'strip', split_axis=0, concat_axis=0, tiled=True)]
    ppermute x28 -> x22, waiting for transfers between devices: 105 us -> 93.7 us  [exchange(): return lax.ppermute(value, axis, [(i, i ^ bit) for i in range(size)])]
    ppermute x4 -> x2, waiting for transfers between devices: 12.9 us -> 3.42 us  [neighbours(): after = lax.ppermute(top, 'strip', down)]
    ppermute x28 -> x22, starting transfers between devices: 32.9 us -> 27.7 us  [exchange(): return lax.ppermute(value, axis, [(i, i ^ bit) for i in range(size)])]
    ppermute x4 -> x2, starting transfers between devices: 6.96 us -> 2.85 us  [neighbours(): before = lax.ppermute(bottom, 'strip', up)]
  transfers between devices with their start and end apart: 40 -> 30, of which waited for: 16 -> 15; matrix products, arithmetic and copies ran while one was open for 1% -> 3% of each run, Pallas kernels for 23% -> 22%
where the time goes in v2:
time: 337 us; the launch traced here: 336 us
  waiting for transfers between devices  145 us (43%)
  Pallas kernels  120 us (36%)
  starting transfers between devices  52.8 us (16%)
  local copies, waits for them, and re-layouts  10.4 us (3%)
  other arithmetic  6.28 us (2%)
    ppermute x22, waiting for transfers between devices, exchange(): return lax.ppermute(value, axis, [(i, i ^ bit) for i in range(size)])  93.7 us
    pallas_call x4, Pallas kernels, pair_sums(): pl.pallas_call(functools.partial(pairs_kernel, k, last, sources, padded),...  66.1 us
    all_to_all x4, waiting for transfers between devices, receive(): lax.all_to_all(piece, 'strip', split_axis=0, concat_axis=0, tiled=True)  48.2 us
    ppermute x22, starting transfers between devices, exchange(): return lax.ppermute(value, axis, [(i, i ^ bit) for i in range(size)])  27.7 us
    pallas_call x2, Pallas kernels, deramp(): pl.pallas_call(functools.partial(deramp_kernel, acqs, chosen, lines is no...  21.1 us
    all_to_all x4, starting transfers between devices, receive(): lax.all_to_all(piece, 'strip', split_axis=0, concat_axis=0, tiled=True)  19.6 us
    pallas_call x4, Pallas kernels, make_tile(): pl.pallas_call(functools.partial(tile_kernel, acqs, padded), grid=(1,), i...  18.4 us
    pallas_call x1, Pallas kernels, finish(): pl.pallas_call(functools.partial(finish_kernel, acqs, padded, groups), gr...  14.7 us
  transfers between devices with their start and end apart: 30, of which 15 were waited for; matrix products, arithmetic and copies ran while one was open for 3% of the time, Pallas kernels for 22%

profile of v2, /device:TPU:0, one launch (start us, length us, event | category | flops | bytes accessed | tf_op | source)
XLA Modules:
  0.0 335.6 jit_solution(17805125463077952464)
XLA Ops:
  0.7 1.6 multiply_sine_fusion
  2.3 9.5 %deramp0.1 = bf16[8,61,16,128]{3,2,1,0:T(8,128)(2,1)} custom-call(f32[30720,128]{1,0:T(8,128)} %bitcast.16, f32[8,16,30]{2,1,0:T(8,128)} %get-tuple-element.72.refs_1_, f32[8,16,30]{2,1,0:T(8,128)} %get-tuple-element.71.refs_2_, s32[8,16]{1,0:T(8,128)} %bitcast.18), custom_call_target="tpu_custom_call" | custom-call | flops 6000000000 | bytes 6000000 | tf_op jit(solution)/shard_map/deramp0/pallas_call | solution.py:100
  11.8 6.3 %all-to-all-start = ((bf16[8,61,16,128]{3,2,1,0:T(8,128)(2,1)}), bf16[8,61,16,128]{3,2,1,0:T(8,128)(2,1)S(1)}, u32[]{:S(2)}, u32[]{:S(2)}) async-start(bf16[8,61,16,128]{3,2,1,0:T(8,128)(2,1)} %deramp0.1), calls=%async_computation | async-start | bytes 3997696 | tf_op jit(solution)/shard_map/all_to_all | solution.py:562
  18.1 11.6 %deramp1.1 = (bf16[8,60,16,128]{3,2,1,0:T(8,128)(2,1)}, bf16[8,60,16,128]{3,2,1,0:T(8,128)(2,1)}, bf16[8,60,16,128]{3,2,1,0:T(8,128)(2,1)}) custom-call(f32[30720,128]{1,0:T(8,128)} %bitcast.17, f32[8,16,30]{2,1,0:T(8,128)} %get-tuple-element.72.refs_1_, f32[8,16,30]{2,1,0:T(8,128)} %get-tuple-element.71.refs_2_), custom_call_target="tpu_custom_call" | custom-call | flops 8999999488 | bytes 9000000 | tf_op jit(solution)/shard_map/deramp1/pallas_call | solution.py:100
  29.8 35.3 %all-to-all-done.lines_ref.data_ref = bf16[8,61,16,128]{3,2,1,0:T(8,128)(2,1)S(1)} async-done(((bf16[8,61,16,128]{3,2,1,0:T(8,128)(2,1)}), bf16[8,61,16,128]{3,2,1,0:T(8,128)(2,1)S(1)}, u32[]{:S(2)}, u32[]{:S(2)}) %all-to-all-start) | async-done | bytes 1998880 | tf_op jit(solution)/shard_map/all_to_all | solution.py:562
  66.4 4.3 %all-to-all-start.1 = ((bf16[8,60,16,128]{3,2,1,0:T(8,128)(2,1)}), bf16[8,60,16,128]{3,2,1,0:T(8,128)(2,1)}, u32[]{:S(2)}, u32[]{:S(2)}) async-start(bf16[8,60,16,128]{3,2,1,0:T(8,128)(2,1)} %get-tuple-element.40), calls=%async_computation.1 | async-start | bytes 3932160 | tf_op jit(solution)/shard_map/all_to_all | solution.py:562
  70.7 4.5 %tile.4 = (bf16[64,64,128]{2,1,0:T(8,128)(2,1)}, bf16[4,64,128]{2,1,0:T(8,128)(2,1)}, bf16[4,64,128]{2,1,0:T(8,128)(2,1)}) custom-call(bf16[8,61,16,128]{3,2,1,0:T(8,128)(2,1)} %copy-done, bf16[8,61,16,128]{3,2,1,0:T(8,128)(2,1)} %copy-done), custom_call_target="tpu_custom_call" | custom-call | flops 4000000000 | bytes 4000000 | tf_op jit(solution)/shard_map/tile/pallas_call | solution.py:153
  78.3 22.6 %collective-permute-done.1.refs_11_.refs_12_ = bf16[64,64,128]{2,1,0:T(8,128)(2,1)S(1)} collective-permute-done((bf16[64,64,128]{2,1,0:T(8,128)(2,1)}, bf16[64,64,128]{2,1,0:T(8,128)(2,1)S(1)}, u32[]{:S(2)}, u32[]{:S(2)}) %collective-permute-start.1) | collective-permute-done | bytes 1048608 | tf_op jit(solution)/shard_map/ppermute | solution.py:494
  102.6 1.6 collective-permute-start.3
  104.2 10.4 %collective-permute-done.2.refs_13_.refs_14_ = bf16[64,32,128]{2,1,0:T(8,128)(2,1)S(1)} collective-permute-done((bf16[64,32,128]{2,1,0:T(8,128)(2,1)S(1)}, bf16[64,32,128]{2,1,0:T(8,128)(2,1)S(1)}, u32[]{:S(2)}, u32[]{:S(2)}) %collective-permute-start.2) | collective-permute-done | bytes 524320 | tf_op jit(solution)/shard_map/ppermute | solution.py:494
  117.0 3.6 %all-to-all-start.2 = ((bf16[8,60,16,128]{3,2,1,0:T(8,128)(2,1)}), bf16[8,60,16,128]{3,2,1,0:T(8,128)(2,1)S(1)}, u32[]{:S(2)}, u32[]{:S(2)}) async-start(bf16[8,60,16,128]{3,2,1,0:T(8,128)(2,1)} %get-tuple-element.42), calls=%async_computation.2 | async-start | bytes 3932160 | tf_op jit(solution)/shard_map/all_to_all | solution.py:562
  120.6 4.5 %tile.6 = (bf16[64,64,128]{2,1,0:T(8,128)(2,1)}, bf16[4,64,128]{2,1,0:T(8,128)(2,1)}, bf16[4,64,128]{2,1,0:T(8,128)(2,1)}) custom-call(bf16[8,61,16,128]{3,2,1,0:T(8,128)(2,1)} %copy-done, bf16[8,60,16,128]{3,2,1,0:T(8,128)(2,1)} %all-to-all-done.1.data_ref), custom_call_target="tpu_custom_call" | custom-call | flops 4000000000 | bytes 4000000 | tf_op jit(solution)/shard_map/tile/pallas_call | solution.py:153
  125.1 1.6 collective-permute-start.7
  128.9 22.0 %collective-permute-done.7.refs_11_.refs_12_ = bf16[64,64,128]{2,1,0:T(8,128)(2,1)S(1)} collective-permute-done((bf16[64,64,128]{2,1,0:T(8,128)(2,1)}, bf16[64,64,128]{2,1,0:T(8,128)(2,1)S(1)}, u32[]{:S(2)}, u32[]{:S(2)}) %collective-permute-start.7) | collective-permute-done | bytes 1048608 | tf_op jit(solution)/shard_map/ppermute | solution.py:494
  155.0 11.8 %all-to-all-done.2.data_ref = bf16[8,60,16,128]{3,2,1,0:T(8,128)(2,1)S(1)} async-done(((bf16[8,60,16,128]{3,2,1,0:T(8,128)(2,1)}), bf16[8,60,16,128]{3,2,1,0:T(8,128)(2,1)S(1)}, u32[]{:S(2)}, u32[]{:S(2)}) %all-to-all-start.2) | async-done | bytes 1966112 | tf_op jit(solution)/shard_map/all_to_all | solution.py:562
  174.6 5.4 %all-to-all-start.3 = ((bf16[8,60,16,128]{3,2,1,0:T(8,128)(2,1)}), bf16[8,60,16,128]{3,2,1,0:T(8,128)(2,1)}, u32[]{:S(2)}, u32[]{:S(2)}) async-start(bf16[8,60,16,128]{3,2,1,0:T(8,128)(2,1)} %get-tuple-element.54), calls=%async_computation.3 | async-start | bytes 3932160 | tf_op jit(solution)/shard_map/all_to_all | solution.py:562
  184.5 4.5 %tile.5 = (bf16[64,64,128]{2,1,0:T(8,128)(2,1)}, bf16[4,64,128]{2,1,0:T(8,128)(2,1)}, bf16[4,64,128]{2,1,0:T(8,128)(2,1)}) custom-call(bf16[8,61,16,128]{3,2,1,0:T(8,128)(2,1)} %copy-done, bf16[8,60,16,128]{3,2,1,0:T(8,128)(2,1)} %copy-done.1), custom_call_target="tpu_custom_call" | custom-call | flops 4000000000 | bytes 4000000 | tf_op jit(solution)/shard_map/tile/pallas_call | solution.py:153
  190.2 6.4 %collective-permute-done.11.refs_5_ = bf16[8,128,128]{2,1,0:T(8,128)(2,1)S(1)} collective-permute-done((bf16[8,128,128]{2,1,0:T(8,128)(2,1)S(1)}, bf16[8,128,128]{2,1,0:T(8,128)(2,1)S(1)}, u32[]{:S(2)}, u32[]{:S(2)}) %collective-permute-start.11) | collective-permute-done | bytes 262176 | tf_op jit(solution)/shard_map/ppermute | solution.py:494
  199.8 15.8 %pairs0.1 = (f32[8,64,64,128]{3,2,1,0:T(8,128)}, f32[72,16,256]{2,1,0:T(8,128)}) custom-call(s32[8]{0:T(128)} %refs_0_.7, f32[8,65,256]{2,1,0:T(8,128)} %and_convert_fusion.refs_1_, f32[65,16,128]{2,1,0:T(8,128)} %broadcast_in_dim.2.refs_2_, bf16[8,128,128]{2,1,0:T(8,128)(2,1)} %copy-done.11, bf16[8,128,128]{2,1,0:T(8,128)(2,1)} %copy-done.31, ...), custom_call_target="tpu_custom_call" | custom-call | flops 16000000000 | bytes 16000000 | tf_op jit(solution)/shard_map/pairs0/pallas_call | solution.py:408
  215.6 6.9 %collective-permute-done.14.refs_11_.refs_12_ = bf16[64,64,128]{2,1,0:T(8,128)(2,1)S(1)} collective-permute-done((bf16[64,64,128]{2,1,0:T(8,128)(2,1)}, bf16[64,64,128]{2,1,0:T(8,128)(2,1)S(1)}, u32[]{:S(2)}, u32[]{:S(2)}) %collective-permute-start.14) | collective-permute-done | bytes 1048608 | tf_op jit(solution)/shard_map/ppermute | solution.py:494
  223.3 1.6 collective-permute-start.16
  224.9 16.7 %pairs1.1 = (f32[8,64,64,128]{3,2,1,0:T(8,128)}, f32[72,16,256]{2,1,0:T(8,128)}) custom-call(s32[8]{0:T(128)} %refs_0_.7, f32[8,65,256]{2,1,0:T(8,128)} %and_convert_fusion.refs_1_, f32[65,16,128]{2,1,0:T(8,128)} %broadcast_in_dim.2.refs_2_, bf16[8,128,128]{2,1,0:T(8,128)(2,1)} %copy-done.11, ...), custom_call_target="tpu_custom_call", output_to_operand_aliasing={{0}: (21, {})} | custom-call | flops 16000000000 | bytes 16000000 | tf_op jit(solution)/shard_map/pairs1/pallas_call | solution.py:408
  241.7 4.8 %tile.7 = (bf16[64,64,128]{2,1,0:T(8,128)(2,1)}, bf16[4,64,128]{2,1,0:T(8,128)(2,1)}, bf16[4,64,128]{2,1,0:T(8,128)(2,1)}) custom-call(bf16[8,61,16,128]{3,2,1,0:T(8,128)(2,1)} %copy-done, bf16[8,60,16,128]{3,2,1,0:T(8,128)(2,1)} %all-to-all-done.3.data_ref), custom_call_target="tpu_custom_call" | custom-call | flops 4000000000 | bytes 4000000 | tf_op jit(solution)/shard_map/tile/pallas_call | solution.py:153
  252.8 3.4 %collective-permute-done.18 = bf16[4,128,128]{2,1,0:T(8,128)(2,1)S(1)} collective-permute-done((bf16[4,128,128]{2,1,0:T(8,128)(2,1)S(1)}, bf16[4,128,128]{2,1,0:T(8,128)(2,1)S(1)}, u32[]{:S(2)}, u32[]{:S(2)}) %collective-permute-start.18) | collective-permute-done | bytes 131104 | tf_op jit(solution)/shard_map/ppermute | solution.py:502
  256.9 1.6 collective-permute-start.20
  259.8 13.1 %collective-permute-done.23.refs_11_.refs_12_ = bf16[64,64,128]{2,1,0:T(8,128)(2,1)S(1)} collective-permute-done((bf16[64,64,128]{2,1,0:T(8,128)(2,1)}, bf16[64,64,128]{2,1,0:T(8,128)(2,1)S(1)}, u32[]{:S(2)}, u32[]{:S(2)}) %collective-permute-start.23) | collective-permute-done | bytes 1048608 | tf_op jit(solution)/shard_map/ppermute | solution.py:494
  275.0 3.9 %collective-permute-done.19.refs_4_ = bf16[8,128,128]{2,1,0:T(8,128)(2,1)S(1)} collective-permute-done((bf16[8,128,128]{2,1,0:T(8,128)(2,1)S(1)}, bf16[8,128,128]{2,1,0:T(8,128)(2,1)S(1)}, u32[]{:S(2)}, u32[]{:S(2)}) %collective-permute-start.19) | collective-permute-done | bytes 262176 | tf_op jit(solution)/shard_map/ppermute | solution.py:494
  279.0 3.7 %collective-permute-done.20.refs_5_ = bf16[8,128,128]{2,1,0:T(8,128)(2,1)S(1)} collective-permute-done((bf16[8,128,128]{2,1,0:T(8,128)(2,1)S(1)}, bf16[8,128,128]{2,1,0:T(8,128)(2,1)S(1)}, u32[]{:S(2)}, u32[]{:S(2)}) %collective-permute-start.20) | collective-permute-done | bytes 262176 | tf_op jit(solution)/shard_map/ppermute | solution.py:494
  282.7 2.9 collective-permute-done.21.refs_6_
  286.3 16.7 %pairs2.1 = (f32[8,64,64,128]{3,2,1,0:T(8,128)}, f32[72,16,256]{2,1,0:T(8,128)}) custom-call(s32[8]{0:T(128)} %refs_0_.7, f32[8,65,256]{2,1,0:T(8,128)} %and_convert_fusion.refs_1_, f32[65,16,128]{2,1,0:T(8,128)} %broadcast_in_dim.2.refs_2_, bf16[8,128,128]{2,1,0:T(8,128)(2,1)} %copy-done.13, ...), custom_call_target="tpu_custom_call", output_to_operand_aliasing={{0}: (21, {})} | custom-call | flops 16000000000 | bytes 16000000 | tf_op jit(solution)/shard_map/pairs2/pallas_call | solution.py:408
  304.0 16.8 %pairs3.1.real_ref.imag_ref.energy_ref = f32[8,64,64,128]{3,2,1,0:T(8,128)} custom-call(s32[8]{0:T(128)} %refs_0_.7, f32[8,65,256]{2,1,0:T(8,128)} %and_convert_fusion.refs_1_, f32[65,16,128]{2,1,0:T(8,128)} %broadcast_in_dim.2.refs_2_, bf16[8,128,128]{2,1,0:T(8,128)(2,1)} %copy-done.13, ...), custom_call_target="tpu_custom_call", output_to_operand_aliasing={{}: (21, {})} | custom-call | flops 16000000000 | bytes 16000000 | tf_op jit(solution)/shard_map/pairs3/pallas_call | solution.py:408
  320.9 14.7 %finish.1 = f32[30,960,128]{2,1,0:T(8,128)} custom-call(s32[1]{0:T(128)} %bitcast.me_ref, f32[8,64,64,128]{3,2,1,0:T(8,128)} %pairs3.1.real_ref.imag_ref.energy_ref, f32[8,64,64,128]{3,2,1,0:T(8,128)} %pairs3.1.real_ref.imag_ref.energy_ref, f32[8,64,64,128]{3,2,1,0:T(8,128)} %pairs3.1.real_ref.imag_ref.energy_ref), custom_call_target="tpu_custom_call" | custom-call | flops 25165824 | bytes 33554432 | tf_op jit(solution)/shard_map/finish/pallas_call | solution.py:470
  (139 shorter events, 44.6 us)
Async XLA Ops:
  11.8 53.3 %all-to-all-start = ((bf16[8,61,16,128]{3,2,1,0:T(8,128)(2,1)}), bf16[8,61,16,128]{3,2,1,0:T(8,128)(2,1)S(1)}, u32[]{:S(2)}, u32[]{:S(2)}) async-start(bf16[8,61,16,128]{3,2,1,0:T(8,128)(2,1)} %deramp0.1), calls=%async_computation | async-start | bytes 3997696 | tf_op jit(solution)/shard_map/all_to_all | solution.py:562
  66.4 50.6 %all-to-all-start.1 = ((bf16[8,60,16,128]{3,2,1,0:T(8,128)(2,1)}), bf16[8,60,16,128]{3,2,1,0:T(8,128)(2,1)}, u32[]{:S(2)}, u32[]{:S(2)}) async-start(bf16[8,60,16,128]{3,2,1,0:T(8,128)(2,1)} %get-tuple-element.40), calls=%async_computation.1 | async-start | bytes 3932160 | tf_op jit(solution)/shard_map/all_to_all | solution.py:562
  75.3 25.6 %collective-permute-start.1 = (bf16[64,64,128]{2,1,0:T(8,128)(2,1)}, bf16[64,64,128]{2,1,0:T(8,128)(2,1)S(1)}, u32[]{:S(2)}, u32[]{:S(2)}) collective-permute-start(bf16[64,64,128]{2,1,0:T(8,128)(2,1)} %get-tuple-element.41.refs_7_.refs_8_.refs_17_.refs_18_), channel_id=1, source_target_pairs={{0,16},{8,24},{16,0},{24,8},{1,17},{9,25},{17,1},{25,9},{2,18},{10... | collective-permute-start | bytes 3145736 | tf_op jit(solution)/shard_map/ppermute | solution.py:494
  76.8 25.7 %collective-permute-start = (bf16[64,64,128]{2,1,0:T(8,128)(2,1)}, bf16[64,64,128]{2,1,0:T(8,128)(2,1)S(1)}, u32[]{:S(2)}, u32[]{:S(2)}) collective-permute-start(bf16[64,64,128]{2,1,0:T(8,128)(2,1)} %get-tuple-element.41.refs_7_.refs_8_.refs_17_.refs_18_), channel_id=1, source_target_pairs={{0,8},{8,0},{16,24},{24,16},{1,9},{9,1},{17,25},{25,17},{2,10},{10... | collective-permute-start | bytes 3145736 | tf_op jit(solution)/shard_map/ppermute | solution.py:494
  101.0 13.5 %collective-permute-start.2 = (bf16[64,32,128]{2,1,0:T(8,128)(2,1)S(1)}, bf16[64,32,128]{2,1,0:T(8,128)(2,1)S(1)}, u32[]{:S(2)}, u32[]{:S(2)}) collective-permute-start(bf16[64,32,128]{2,1,0:T(8,128)(2,1)S(1)} %slice.32), channel_id=1, source_target_pairs={{0,8},{8,0},{16,24},{24,16},{1,9},{9,1},{17,25},{25,17},{2,10},{10... | collective-permute-start | bytes 1572872 | tf_op jit(solution)/shard_map/ppermute | solution.py:494
  102.6 13.4 %collective-permute-start.3 = (bf16[64,32,128]{2,1,0:T(8,128)(2,1)S(1)}, bf16[64,32,128]{2,1,0:T(8,128)(2,1)}, u32[]{:S(2)}, u32[]{:S(2)}) collective-permute-start(bf16[64,32,128]{2,1,0:T(8,128)(2,1)S(1)} %slice.33), channel_id=1, source_target_pairs={{0,16},{8,24},{16,0},{24,8},{1,17},{9,25},{17,1},{25,9},{2,18},{10... | collective-permute-start | bytes 1572872 | tf_op jit(solution)/shard_map/ppermute | solution.py:494
  117.0 49.8 %all-to-all-start.2 = ((bf16[8,60,16,128]{3,2,1,0:T(8,128)(2,1)}), bf16[8,60,16,128]{3,2,1,0:T(8,128)(2,1)S(1)}, u32[]{:S(2)}, u32[]{:S(2)}) async-start(bf16[8,60,16,128]{3,2,1,0:T(8,128)(2,1)} %get-tuple-element.42), calls=%async_computation.2 | async-start | bytes 3932160 | tf_op jit(solution)/shard_map/all_to_all | solution.py:562
  125.1 43.3 %copy-start.15 = (bf16[4,64,128]{2,1,0:T(8,128)(2,1)S(1)}, bf16[4,64,128]{2,1,0:T(8,128)(2,1)}, u32[]{:S(2)}) copy-start(bf16[4,64,128]{2,1,0:T(8,128)(2,1)} %get-tuple-element.50) | copy-start | bytes 196612
  125.1 43.3 %copy-start.18 = (bf16[4,64,128]{2,1,0:T(8,128)(2,1)S(1)}, bf16[4,64,128]{2,1,0:T(8,128)(2,1)}, u32[]{:S(2)}) copy-start(bf16[4,64,128]{2,1,0:T(8,128)(2,1)} %get-tuple-element.52) | copy-start | bytes 196612
  125.1 25.8 %collective-permute-start.7 = (bf16[64,64,128]{2,1,0:T(8,128)(2,1)}, bf16[64,64,128]{2,1,0:T(8,128)(2,1)S(1)}, u32[]{:S(2)}, u32[]{:S(2)}) collective-permute-start(bf16[64,64,128]{2,1,0:T(8,128)(2,1)} %get-tuple-element.53.refs_7_.refs_8_.refs_17_.refs_18_), channel_id=1, source_target_pairs={{0,16},{8,24},{16,0},{24,8},{1,17},{9,25},{17,1},{25,9},{2,18},{10... | collective-permute-start | bytes 3145736 | tf_op jit(solution)/shard_map/ppermute | solution.py:494
  126.7 25.8 %collective-permute-start.6 = (bf16[64,64,128]{2,1,0:T(8,128)(2,1)}, bf16[64,64,128]{2,1,0:T(8,128)(2,1)S(1)}, u32[]{:S(2)}, u32[]{:S(2)}) collective-permute-start(bf16[64,64,128]{2,1,0:T(8,128)(2,1)} %get-tuple-element.53.refs_7_.refs_8_.refs_17_.refs_18_), channel_id=1, source_target_pairs={{0,8},{8,0},{16,24},{24,16},{1,9},{9,1},{17,25},{25,17},{2,10},{10... | collective-permute-start | bytes 3145736 | tf_op jit(solution)/shard_map/ppermute | solution.py:494
  150.9 23.0 %collective-permute-start.8 = (bf16[64,32,128]{2,1,0:T(8,128)(2,1)S(1)}, bf16[64,32,128]{2,1,0:T(8,128)(2,1)}, u32[]{:S(2)}, u32[]{:S(2)}) collective-permute-start(bf16[64,32,128]{2,1,0:T(8,128)(2,1)S(1)} %slice.34), channel_id=1, source_target_pairs={{0,8},{8,0},{16,24},{24,16},{1,9},{9,1},{17,25},{25,17},{2,10},{10... | collective-permute-start | bytes 1572872 | tf_op jit(solution)/shard_map/ppermute | solution.py:494
  153.5 20.4 %collective-permute-start.9 = (bf16[64,32,128]{2,1,0:T(8,128)(2,1)S(1)}, bf16[64,32,128]{2,1,0:T(8,128)(2,1)}, u32[]{:S(2)}, u32[]{:S(2)}) collective-permute-start(bf16[64,32,128]{2,1,0:T(8,128)(2,1)S(1)} %slice.35), channel_id=1, source_target_pairs={{0,16},{8,24},{16,0},{24,8},{1,17},{9,25},{17,1},{25,9},{2,18},{10... | collective-permute-start | bytes 1572872 | tf_op jit(solution)/shard_map/ppermute | solution.py:494
  166.8 7.1 %collective-permute-start.4 = (bf16[4,128,128]{2,1,0:T(8,128)(2,1)S(1)}, bf16[4,128,128]{2,1,0:T(8,128)(2,1)S(1)}, u32[]{:S(2)}, u32[]{:S(2)}) collective-permute-start(bf16[4,128,128]{2,1,0:T(8,128)(2,1)S(1)} %pad_maximum_fusion), channel_id=1, source_target_pairs={{0,1},{1,2},{2,3},{3,4},{4,5},{5,6},{6,7},{8,9},{9,10},{10,11},{11... | collective-permute-start | bytes 393224 | tf_op jit(solution)/shard_map/ppermute | solution.py:501
  168.4 5.5 %collective-permute-start.5 = (bf16[4,128,128]{2,1,0:T(8,128)(2,1)S(1)}, bf16[4,128,128]{2,1,0:T(8,128)(2,1)S(1)}, u32[]{:S(2)}, u32[]{:S(2)}) collective-permute-start(bf16[4,128,128]{2,1,0:T(8,128)(2,1)S(1)} %pad_maximum_fusion.1), channel_id=1, source_target_pairs={{1,0},{2,1},{3,2},{4,3},{5,4},{6,5},{7,6},{9,8},{10,9},{11,10},{12... | collective-permute-start | bytes 393224 | tf_op jit(solution)/shard_map/ppermute | solution.py:502
  174.6 67.0 %all-to-all-start.3 = ((bf16[8,60,16,128]{3,2,1,0:T(8,128)(2,1)}), bf16[8,60,16,128]{3,2,1,0:T(8,128)(2,1)}, u32[]{:S(2)}, u32[]{:S(2)}) async-start(bf16[8,60,16,128]{3,2,1,0:T(8,128)(2,1)} %get-tuple-element.54), calls=%async_computation.3 | async-start | bytes 3932160 | tf_op jit(solution)/shard_map/all_to_all | solution.py:562
  181.0 9.2 %collective-permute-start.10 = (bf16[8,128,128]{2,1,0:T(8,128)(2,1)S(1)}, bf16[8,128,128]{2,1,0:T(8,128)(2,1)S(1)}, u32[]{:S(2)}, u32[]{:S(2)}) collective-permute-start(bf16[8,128,128]{2,1,0:T(8,128)(2,1)S(1)} %copy-done.12), channel_id=1, source_target_pairs={{0,8},{8,0},{16,24},{24,16},{1,9},{9,1},{17,25},{25,17},{2,10},{10... | collective-permute-start | bytes 786440 | tf_op jit(solution)/shard_map/ppermute | solution.py:494
  182.6 14.0 %collective-permute-start.11 = (bf16[8,128,128]{2,1,0:T(8,128)(2,1)S(1)}, bf16[8,128,128]{2,1,0:T(8,128)(2,1)S(1)}, u32[]{:S(2)}, u32[]{:S(2)}) collective-permute-start(bf16[8,128,128]{2,1,0:T(8,128)(2,1)S(1)} %copy-done.12), channel_id=1, source_target_pairs={{0,16},{8,24},{16,0},{24,8},{1,17},{9,25},{17,1},{25,9},{2,18},{10... | collective-permute-start | bytes 786440 | tf_op jit(solution)/shard_map/ppermute | solution.py:494
  184.1 12.5 %collective-permute-start.12 = (bf16[8,128,128]{2,1,0:T(8,128)(2,1)S(1)}, bf16[8,128,128]{2,1,0:T(8,128)(2,1)S(1)}, u32[]{:S(2)}, u32[]{:S(2)}) collective-permute-start(bf16[8,128,128]{2,1,0:T(8,128)(2,1)S(1)} %copy-done.12), channel_id=1, source_target_pairs={{0,24},{8,16},{16,8},{24,0},{1,25},{9,17},{17,9},{25,1},{2,26},{10... | collective-permute-start | bytes 786440 | tf_op jit(solution)/shard_map/ppermute | solution.py:494
  196.6 26.6 %collective-permute-start.13 = (bf16[64,64,128]{2,1,0:T(8,128)(2,1)}, bf16[64,64,128]{2,1,0:T(8,128)(2,1)S(1)}, u32[]{:S(2)}, u32[]{:S(2)}) collective-permute-start(bf16[64,64,128]{2,1,0:T(8,128)(2,1)} %get-tuple-element.59.refs_7_.refs_8_.refs_17_.refs_18_), channel_id=1, source_target_pairs={{0,8},{8,0},{16,24},{24,16},{1,9},{9,1},{17,25},{25,17},{2,10},{10... | collective-permute-start | bytes 3145736 | tf_op jit(solution)/shard_map/ppermute | solution.py:494
  197.8 24.7 %collective-permute-start.14 = (bf16[64,64,128]{2,1,0:T(8,128)(2,1)}, bf16[64,64,128]{2,1,0:T(8,128)(2,1)S(1)}, u32[]{:S(2)}, u32[]{:S(2)}) collective-permute-start(bf16[64,64,128]{2,1,0:T(8,128)(2,1)} %get-tuple-element.59.refs_7_.refs_8_.refs_17_.refs_18_), channel_id=1, source_target_pairs={{0,16},{8,24},{16,0},{24,8},{1,17},{9,25},{17,1},{25,9},{2,18},{10... | collective-permute-start | bytes 3145736 | tf_op jit(solution)/shard_map/ppermute | solution.py:494
  222.6 19.1 %collective-permute-start.15 = (bf16[64,32,128]{2,1,0:T(8,128)(2,1)S(1)}, bf16[64,32,128]{2,1,0:T(8,128)(2,1)S(1)}, u32[]{:S(2)}, u32[]{:S(2)}) collective-permute-start(bf16[64,32,128]{2,1,0:T(8,128)(2,1)S(1)} %slice.36), channel_id=1, source_target_pairs={{0,8},{8,0},{16,24},{24,16},{1,9},{9,1},{17,25},{25,17},{2,10},{10... | collective-permute-start | bytes 1572872 | tf_op jit(solution)/shard_map/ppermute | solution.py:494
  223.3 18.4 %collective-permute-start.16 = (bf16[64,32,128]{2,1,0:T(8,128)(2,1)S(1)}, bf16[64,32,128]{2,1,0:T(8,128)(2,1)S(1)}, u32[]{:S(2)}, u32[]{:S(2)}) collective-permute-start(bf16[64,32,128]{2,1,0:T(8,128)(2,1)S(1)} %slice.37), channel_id=1, source_target_pairs={{0,16},{8,24},{16,0},{24,8},{1,17},{9,25},{17,1},{25,9},{2,18},{10... | collective-permute-start | bytes 1572872 | tf_op jit(solution)/shard_map/ppermute | solution.py:494
  246.5 26.4 %collective-permute-start.23 = (bf16[64,64,128]{2,1,0:T(8,128)(2,1)}, bf16[64,64,128]{2,1,0:T(8,128)(2,1)S(1)}, u32[]{:S(2)}, u32[]{:S(2)}) collective-permute-start(bf16[64,64,128]{2,1,0:T(8,128)(2,1)} %get-tuple-element.67.refs_7_.refs_8_), channel_id=1, source_target_pairs={{0,16},{8,24},{16,0},{24,8},{1,17},{9,25},{17,1},{25,9},{2,18},{10... | collective-permute-start | bytes 3145736 | tf_op jit(solution)/shard_map/ppermute | solution.py:494
  247.0 26.4 %collective-permute-start.22 = (bf16[64,64,128]{2,1,0:T(8,128)(2,1)}, bf16[64,64,128]{2,1,0:T(8,128)(2,1)S(1)}, u32[]{:S(2)}, u32[]{:S(2)}) collective-permute-start(bf16[64,64,128]{2,1,0:T(8,128)(2,1)} %get-tuple-element.67.refs_7_.refs_8_), channel_id=1, source_target_pairs={{0,8},{8,0},{16,24},{24,16},{1,9},{9,1},{17,25},{25,17},{2,10},{10... | collective-permute-start | bytes 3145736 | tf_op jit(solution)/shard_map/ppermute | solution.py:494
  249.3 3.5 %collective-permute-start.17 = (bf16[4,128,128]{2,1,0:T(8,128)(2,1)S(1)}, bf16[4,128,128]{2,1,0:T(8,128)(2,1)S(1)}, u32[]{:S(2)}, u32[]{:S(2)}) collective-permute-start(bf16[4,128,128]{2,1,0:T(8,128)(2,1)S(1)} %pad_maximum_fusion.2), channel_id=1, source_target_pairs={{0,1},{1,2},{2,3},{3,4},{4,5},{5,6},{6,7},{8,9},{9,10},{10,11},{11... | collective-permute-start | bytes 393224 | tf_op jit(solution)/shard_map/ppermute | solution.py:501
  251.5 4.7 %collective-permute-start.18 = (bf16[4,128,128]{2,1,0:T(8,128)(2,1)S(1)}, bf16[4,128,128]{2,1,0:T(8,128)(2,1)S(1)}, u32[]{:S(2)}, u32[]{:S(2)}) collective-permute-start(bf16[4,128,128]{2,1,0:T(8,128)(2,1)S(1)} %pad_maximum_fusion.3), channel_id=1, source_target_pairs={{1,0},{2,1},{3,2},{4,3},{5,4},{6,5},{7,6},{9,8},{10,9},{11,10},{12... | collective-permute-start | bytes 393224 | tf_op jit(solution)/shard_map/ppermute | solution.py:502
  256.3 22.7 %collective-permute-start.19 = (bf16[8,128,128]{2,1,0:T(8,128)(2,1)S(1)}, bf16[8,128,128]{2,1,0:T(8,128)(2,1)S(1)}, u32[]{:S(2)}, u32[]{:S(2)}) collective-permute-start(bf16[8,128,128]{2,1,0:T(8,128)(2,1)S(1)} %constant_dynamic-update-slice_fusion.2.refs_3_.refs_19_), channel_id=1, source_target_pairs={{0,8},{8,0},{16,24},{24,16},{1,9},{9,1},{17,25},{25,17},{2,10},{10... | collective-permute-start | bytes 786440 | tf_op jit(solution)/shard_map/ppermute | solution.py:494
  256.9 25.7 %collective-permute-start.20 = (bf16[8,128,128]{2,1,0:T(8,128)(2,1)S(1)}, bf16[8,128,128]{2,1,0:T(8,128)(2,1)S(1)}, u32[]{:S(2)}, u32[]{:S(2)}) collective-permute-start(bf16[8,128,128]{2,1,0:T(8,128)(2,1)S(1)} %constant_dynamic-update-slice_fusion.2.refs_3_.refs_19_), channel_id=1, source_target_pairs={{0,16},{8,24},{16,0},{24,8},{1,17},{9,25},{17,1},{25,9},{2,18},{10... | collective-permute-start | bytes 786440 | tf_op jit(solution)/shard_map/ppermute | solution.py:494
  258.5 27.1 %collective-permute-start.21 = (bf16[8,128,128]{2,1,0:T(8,128)(2,1)S(1)}, bf16[8,128,128]{2,1,0:T(8,128)(2,1)S(1)}, u32[]{:S(2)}, u32[]{:S(2)}) collective-permute-start(bf16[8,128,128]{2,1,0:T(8,128)(2,1)S(1)} %constant_dynamic-update-slice_fusion.2.refs_3_.refs_19_), channel_id=1, source_target_pairs={{0,24},{8,16},{16,8},{24,0},{1,25},{9,17},{17,9},{25,1},{2,26},{10... | collective-permute-start | bytes 786440 | tf_op jit(solution)/shard_map/ppermute | solution.py:494
  273.0 30.0 %collective-permute-start.24 = (bf16[64,32,128]{2,1,0:T(8,128)(2,1)S(1)}, bf16[64,32,128]{2,1,0:T(8,128)(2,1)S(1)}, u32[]{:S(2)}, u32[]{:S(2)}) collective-permute-start(bf16[64,32,128]{2,1,0:T(8,128)(2,1)S(1)} %slice.38), channel_id=1, source_target_pairs={{0,8},{8,0},{16,24},{24,16},{1,9},{9,1},{17,25},{25,17},{2,10},{10... | collective-permute-start | bytes 1572872 | tf_op jit(solution)/shard_map/ppermute | solution.py:494
  273.5 29.6 %collective-permute-start.25 = (bf16[64,32,128]{2,1,0:T(8,128)(2,1)S(1)}, bf16[64,32,128]{2,1,0:T(8,128)(2,1)S(1)}, u32[]{:S(2)}, u32[]{:S(2)}) collective-permute-start(bf16[64,32,128]{2,1,0:T(8,128)(2,1)S(1)} %slice.39), channel_id=1, source_target_pairs={{0,16},{8,24},{16,0},{24,8},{1,17},{9,25},{17,1},{25,9},{2,18},{10... | collective-permute-start | bytes 1572872 | tf_op jit(solution)/shard_map/ppermute | solution.py:494
  (33 other events, 329.4 us)
